TPU v7x, 512 devices: a whole 4x4x16 slice. The times are simulated.
512 devices in a mesh: blk: 8 (over y, core), sp: 64 (over z, x).
Axes of the slice: x: 4, y: 4, z: 16, core: 2. Of those that a mesh axis runs over, the one named last changes fastest.
Arguments:
- snapshots: float32 [64, 256, 32768], P('blk', None, 'sp'), may hold values from -6 to 6
- weights: float32 [32768], P('sp'), may hold values from 0.25 to 4
- counts: int32 [128], P('blk'), may hold values from 1 to 16
Outputs:
- modes: bfloat16 [128, 2, 16, 32768], P('blk', None, None, 'sp')
- values: float32 [128, 16], P('blk')
All inputs are finite; a program needn't handle non-finite values.
Results may differ from a plain program's by a relative error of at most 0.01.
Values may be sent and summed in bfloat16 or wider, within the bound.
No kernel may reach another device: no remote copies, remote signals or barrier semaphores. Data moves between devices by JAX's collectives and lax.ppermute only.
A program may use at most 64 MiB of HBM per device.

v0:
```python
import jax
import jax.numpy as jnp
from jax import lax
from jax.sharding import PartitionSpec as P

KM = 16
ITERS = 3


def make_table(freqs, steps):
    times = jnp.arange(steps, dtype=jnp.int32)
    rows = jnp.arange(freqs, dtype=jnp.int32)
    phase = (rows[:, None] * times[None, :] % steps).astype(jnp.float32)
    angle = 2.0 * jnp.pi * phase / steps
    window = (
        jnp.sqrt(8.0 / (3.0 * steps))
        * 0.5
        * (1.0 - jnp.cos(2.0 * jnp.pi * times.astype(jnp.float32) / steps))
    )
    return jnp.stack([jnp.cos(angle) * window, -jnp.sin(angle) * window], 1)


def gram_pieces(band_spec, weights):
    weighted = (band_spec.astype(jnp.float32) * weights).astype(jnp.bfloat16)
    flipped = jnp.stack([band_spec[:, :, 1], -band_spec[:, :, 0]], 2)
    gram_real = jnp.einsum(
        "bfcp,dfcp->fbd", weighted, band_spec, preferred_element_type=jnp.float32
    )
    gram_imag = jnp.einsum("bfcp,dfcp->fbd", weighted, flipped, preferred_element_type=jnp.float32)
    return jnp.stack([gram_real, gram_imag], 0)


def local(snapshots, weights, counts):
    blk_dev, steps, pts = snapshots.shape
    groups = lax.axis_size("blk")
    band = counts.shape[0]
    freqs = band * groups
    blocks = blk_dev * groups
    points_all = pts * lax.axis_size("sp")
    high = lax.Precision.HIGHEST
    table = make_table(freqs, steps)
    spectra = jnp.einsum("fct,btp->bfcp", table, snapshots, precision=high).astype(jnp.bfloat16)
    shaped = spectra.reshape(blk_dev, groups, band, 2, pts)
    own = lax.all_to_all(shaped, "blk", split_axis=1, concat_axis=0, tiled=True)[:, 0]
    partial_value = gram_pieces(own, weights)
    total = lax.psum(partial_value, "sp") / points_all
    gram_real = total[0]
    gram_imag = total[1]
    upper = jnp.concatenate([gram_real, -gram_imag], 2)
    lower_rows = jnp.concatenate([gram_imag, gram_real], 2)
    embedded = jnp.concatenate([upper, lower_rows], 1)
    kept = KM
    basis = embedded[:, :, :kept]
    for step in range(ITERS):
        image = jnp.einsum("fij,fjk->fik", embedded, basis, precision=high)
        cross = jnp.einsum("fik,fil->fkl", image, image, precision=high)
        factor = jnp.linalg.cholesky(cross)
        basis = jnp.swapaxes(
            jax.scipy.linalg.solve_triangular(factor, jnp.swapaxes(image, 1, 2), lower=True), 1, 2
        )
    quotient = jnp.sum(basis * jnp.einsum("fij,fjk->fik", embedded, basis, precision=high), 1)
    coef = basis.astype(jnp.bfloat16)
    coef_re = coef[:, :blocks]
    coef_im = coef[:, blocks:]
    from_real = jnp.stack([coef_re, coef_im], 2)
    from_imag = jnp.stack([-coef_im, coef_re], 2)
    combined = jnp.stack([from_real, from_imag], 1)
    field = jnp.einsum("bfcp,fcbqk->fqkp", own, combined, preferred_element_type=jnp.float32)
    local_energy = jnp.sum(weights * jnp.sum(field * field, 1), 2)
    energy = lax.psum(local_energy, "sp") / points_all
    keep = jnp.arange(kept, dtype=jnp.int32)[None, :] < counts[:, None]
    scale = jnp.where(keep, 1.0 / jnp.sqrt(energy + 1e-06), 0.0)
    modes = (field * scale[:, None, :, None]).astype(jnp.bfloat16)
    return (modes, jnp.where(keep, quotient, 0.0))


def solution(mesh):
    in_specs = (P("blk", None, "sp"), P("sp"), P("blk"))
    out_specs = (P("blk", None, None, "sp"), P("blk", None))
    return jax.shard_map(local, mesh=mesh, in_specs=in_specs, out_specs=out_specs, check_vma=False)
```

profile of v0, /device:TPU:8, one launch (start us, length us, event | category | flops | bytes accessed | tf_op | source)
XLA Modules:
  0.0 628.9 jit_solution(3678438918512707688)
XLA Ops:
  7.8 6.8 %fusion.11 = bf16[128,2,8,512]{3,0,2,1:T(8,128)(2,1)S(1)} fusion(f32[8,256,512]{2,1,0:T(8,128)} %param.6, f32[128,1,256]{2,0,1:T(8,128)S(1)} %get-tuple-element.18, f32[128,1,256]{2,0,1:T(8,128)S(1)} %get-tuple-element.17), kind=kOutput, calls=%fused_computation.12 | convolution fusion | flops 3222339584 | bytes 6553600 | tf_op jit(solution)/shard_map/fct,btp->bfcp/dot_general | solution.py:42
  14.9 34.3 %all_to_all.15 = bf16[8,8,16,2,512]{4,2,0,3,1:T(8,128)(2,1)S(1)} all-to-all(bf16[8,8,16,2,512]{4,2,0,3,1:T(8,128)(2,1)S(1)} %copy.20), channel_id=1, replica_groups=mesh['blk'=8,'sp'=64] {'blk'}, dimensions={1} | all-to-all | bytes 4194304 | tf_op jit(solution)/shard_map/all_to_all | solution.py:44
  49.2 1.2 copy.57
  51.0 2.3 fusion.17
  53.4 1.4 fusion.14
  54.8 1.1 pad_maximum_fusion
  55.9 273.2 %all-reduce.2.cloned.1.call-done = f32[2,16,64,64]{3,2,1,0:T(8,128)} async-done(((f32[2,16,64,64]{3,2,1,0:T(8,128)}), f32[2,16,64,64]{3,2,1,0:T(8,128)}) %all-reduce.2.cloned.1.call-update) | async-done | bytes 524304 | tf_op jit(solution)/shard_map/psum | solution.py:46
  329.1 1.3 broadcast_multiply_fusion
  330.9 1.8 fusion.19
  333.1 0.7 fusion.40
  333.8 24.1 %custom-call.10 = f32[16,16,16]{2,1,0:T(8,128)S(1)} custom-call(f32[16,16,16]{2,1,0:T(8,128)} %fusion.40), custom_call_target="Cholesky" | custom-call | tf_op jit(solution)/shard_map/jit(cholesky)/cholesky | solution.py:57
  358.2 19.8 %custom-call.11 = f32[16,1,16,16]{2,3,1,0:T(8,128)S(1)} custom-call(f32[16,1,16,16]{3,2,1,0:T(8,128)S(1)} %select_bitcast_fusion.2), custom_call_target="InvertDiagBlocksLowerTriangular" | custom-call | tf_op jit(solution)/shard_map/jit(_solve_triangular)/vmap()/triangular_solve | solution.py:59
  378.5 1.7 fusion.50
  381.3 24.1 %custom-call.12 = f32[16,16,16]{2,1,0:T(8,128)S(1)} custom-call(f32[16,16,16]{2,1,0:T(8,128)} %fusion.36), custom_call_target="Cholesky" | custom-call | tf_op jit(solution)/shard_map/jit(cholesky)/cholesky | solution.py:57
  405.7 19.8 %custom-call.13 = f32[16,1,16,16]{2,3,1,0:T(8,128)S(1)} custom-call(f32[16,1,16,16]{3,2,1,0:T(8,128)S(1)} %select_bitcast_fusion.1), custom_call_target="InvertDiagBlocksLowerTriangular" | custom-call | tf_op jit(solution)/shard_map/jit(_solve_triangular)/vmap()/triangular_solve | solution.py:59
  425.9 1.7 fusion.52
  428.8 24.1 %custom-call.14 = f32[16,16,16]{2,1,0:T(8,128)S(1)} custom-call(f32[16,16,16]{2,1,0:T(8,128)} %fusion.32), custom_call_target="Cholesky" | custom-call | tf_op jit(solution)/shard_map/jit(cholesky)/cholesky | solution.py:57
  453.1 0.7 select_bitcast_fusion
  453.8 20.4 %custom-call.15 = f32[16,1,16,16]{2,3,1,0:T(8,128)S(1)} custom-call(f32[16,1,16,16]{3,2,1,0:T(8,128)} %select_bitcast_fusion), custom_call_target="InvertDiagBlocksLowerTriangular" | custom-call | tf_op jit(solution)/shard_map/jit(_solve_triangular)/vmap()/triangular_solve | solution.py:59
  475.4 1.0 copy-done
  476.6 141.9 %psum.15 = f32[16,16]{1,0:T(8,128)S(1)} all-reduce(f32[16,16]{1,0:T(8,128)S(1)} %multiply_reduce_fusion), channel_id=1, replica_groups=mesh['blk'=8,'sp'=64] {'sp'}, use_global_device_ids=true, to_apply=%region_5.8 | all-reduce | flops 256 | bytes 2048 | tf_op jit(solution)/shard_map/psum | solution.py:70
  618.5 1.8 fusion.18
  620.3 0.7 fusion.44
  621.2 0.8 copy.30
  (42 shorter events, 7.7 us)
Async XLA Ops:
  7.2 322.0 %all-reduce.2.cloned.1.call-start = ((), (), s32[]{:S(2)}) async-start(), calls=%async_computation.1 | async-start | bytes 2097152 | tf_op jit(solution)/shard_map/psum | solution.py:46
  50.3 0.7 copy-start.2
  475.4 1.0 copy-start
  476.4 144.0 %copy-start.3 = (s32[16]{0:T(128)S(1)}, s32[16]{0:T(128)}, u32[]{:S(2)}) copy-start(s32[16]{0:T(128)} %param.8) | copy-start | bytes 196
  476.5 144.5 %copy-start.1 = (f32[16,2,16,512,1]{3,2,1,0,4:T(8,128)S(1)}, f32[16,2,16,512,1]{3,2,1,0,4:T(8,128)}, u32[]{:S(2)}) copy-start(f32[16,2,16,512,1]{3,2,1,0,4:T(8,128)} %copy-done) | copy-start | bytes 3145732
Sparse Core Ops, SparseCore 0:
  56.0 273.0 all-reduce.1
where the time goes:
time: 629 us
  waiting for transfers between devices  273 us (43%)
  blocking collectives  176 us (28%)
  other arithmetic  141 us (22%)
  matrix products  20.4 us (3%)
  between operations  14.3 us (2%)
    psum x1, waiting for transfers between devices, local(): total = lax.psum(partial_value, 'sp') / points_all  273 us
    psum x1, blocking collectives, local(): energy = lax.psum(local_energy, 'sp') / points_all  142 us
    another operation x9, other arithmetic, local(): factor = jnp.linalg.cholesky(cross)  72.7 us
    another operation x7, other arithmetic, local(): jax.scipy.linalg.solve_triangular(factor, jnp.swapaxes(image, 1, 2), lowe...  61 us
    all_to_all x1, blocking collectives, local(): lax.all_to_all(shaped, 'blk', split_axis=1, concat_axis=0, tiled=True)[:, 0]  34.3 us
  transfers between devices with their start and end apart: 1, of which 1 were waited for; matrix products, arithmetic and copies ran while one was open for 0% of the time, Pallas kernels for 0%

commit v1 on v0

v1 whole, which is shorter than its diff:
```python
import functools

import jax
import jax.numpy as jnp
import ml_dtypes
import numpy as np
from jax import lax
from jax.experimental import pallas as pl
from jax.experimental.pallas import tpu as pltpu
from jax.sharding import PartitionSpec as P

KM = 16
F32 = jnp.float32
BF16 = jnp.bfloat16
NN = (((1,), (0,)), ((), ()))
NT = (((1,), (1,)), ((), ()))
VMEM_LIMIT = 48 * 1024 * 1024


def make_table(freqs, steps):
    times = np.arange(steps)
    phase = (np.arange(freqs)[:, None] * times[None, :]) % steps
    angle = 2.0 * np.pi * phase / steps
    window = np.sqrt(8.0 / (3.0 * steps)) * 0.5 * (1.0 - np.cos(2.0 * np.pi * times / steps))
    table = np.stack([np.cos(angle) * window, np.sin(angle) * window], 1)
    table = table.reshape(2 * freqs, steps).astype(np.float32)
    high = table.astype(ml_dtypes.bfloat16)
    low = (table - high.astype(np.float32)).astype(ml_dtypes.bfloat16)
    return high, low


def split(x):
    high = x.astype(BF16)
    return high, (x - high.astype(F32)).astype(BF16)


def mm(a, b, dims=NN, precision=None):
    return lax.dot_general(a, b, dims, preferred_element_type=F32, precision=precision)


def dft_kernel(high_ref, low_ref, x_ref, out_ref, acc_ref):
    blocks = x_ref.shape[0]
    rows = high_ref.shape[0]
    high, low = high_ref[...], low_ref[...]
    for b in range(blocks):
        xh, xl = split(x_ref[b])
        acc = mm(high, xh) + mm(high, xl) + mm(low, xh)
        for col in range(0, acc.shape[1], 128):
            acc_ref[col // 128, pl.ds(b, rows, stride=blocks), :] = acc[:, col : col + 128]
    for col in range(0, out_ref.shape[1], 128):
        out_ref[:, col : col + 128] = acc_ref[col // 128].astype(BF16)


def dft(snapshots, freqs):
    blocks, steps, pts = snapshots.shape
    high, low = make_table(freqs, steps)
    wide = 256
    rows = 2 * freqs
    return pl.pallas_call(
        dft_kernel,
        grid=(pts // wide,),
        in_specs=[
            pl.BlockSpec((rows, steps), lambda i: (0, 0)),
            pl.BlockSpec((rows, steps), lambda i: (0, 0)),
            pl.BlockSpec((blocks, steps, wide), lambda i: (0, 0, i)),
        ],
        out_specs=pl.BlockSpec((rows * blocks, wide), lambda i: (0, i)),
        out_shape=jax.ShapeDtypeStruct((rows * blocks, pts), BF16),
        scratch_shapes=[pltpu.VMEM((wide // 128, rows * blocks, 128), F32)],
        compiler_params=pltpu.CompilerParams(vmem_limit_bytes=VMEM_LIMIT),
        name="dft",
    )(jnp.asarray(high), jnp.asarray(low), snapshots)


def exchange(x, sign_first):
    lane = lax.broadcasted_iota(jnp.int32, x.shape, x.ndim - 1)
    last = x.ndim - 1
    up = pltpu.roll(x, 120, last)
    down = pltpu.roll(x, 8, last)
    if sign_first:
        return jnp.where((lane & 8) == 0, -up, down)
    return jnp.where((lane & 8) == 0, up, -down)


def gram_kernel(points_all, z_ref, w_ref, out_ref):
    groups, freqs, pairs, pts = z_ref.shape
    weights = w_ref[...]
    for f in range(freqs):
        z = z_ref[:, f].reshape(groups * pairs, pts)
        zw = (z.astype(F32) * weights).astype(BF16)
        m = mm(zw, z, NT).reshape(groups, 2, pairs // 2, 128)
        top = m[:, 0].reshape(groups * pairs // 2, 128)
        bottom = m[:, 1].reshape(groups * pairs // 2, 128)
        out_ref[f] = (top + exchange(bottom, False)) * (1.0 / points_all)


def gram(own, weights, points_all):
    groups, freqs, pairs, pts = own.shape
    return pl.pallas_call(
        functools.partial(gram_kernel, points_all),
        in_specs=[pl.BlockSpec(memory_space=pltpu.VMEM)] * 2,
        out_specs=pl.BlockSpec(memory_space=pltpu.VMEM),
        out_shape=jax.ShapeDtypeStruct((freqs, groups * pairs // 2, 128), F32),
        compiler_params=pltpu.CompilerParams(vmem_limit_bytes=VMEM_LIMIT),
        name="gram",
    )(own, weights.reshape(1, pts))


def inverse_factor(cross):
    row = lax.broadcasted_iota(jnp.int32, cross.shape, 0)
    lane = lax.broadcasted_iota(jnp.int32, cross.shape, 1)
    inv = jnp.where((lane & (KM - 1)) == row, 1.0, 0.0)
    pivots = jnp.ones_like(cross)
    for k in range(KM):
        column = jnp.take_along_axis(cross, (lane & ~(KM - 1)) + k, axis=1)
        pivot = jnp.broadcast_to(column[k : k + 1], cross.shape)
        pivots = jnp.where(row == k, pivot, pivots)
        if k < KM - 1:
            factor = jnp.where(row > k, column / pivot, 0.0)
            cross = cross - factor * cross[k : k + 1]
            inv = inv - factor * inv[k : k + 1]
    return inv * lax.rsqrt(pivots)


def orthonormal(image):
    high = lax.Precision.HIGHEST
    product = mm(image, image, NT, high)
    lane = lax.broadcasted_iota(jnp.int32, (KM, 128), 1)
    cross = jnp.zeros((KM, 128), F32)
    for f in range(128 // KM):
        cross = jnp.where(lane // KM == f, product[f * KM : (f + 1) * KM], cross)
    inv = inverse_factor(cross)
    wide = jnp.concatenate([inv] * (128 // KM), 0)
    row = lax.broadcasted_iota(jnp.int32, wide.shape, 0)
    column = lax.broadcasted_iota(jnp.int32, wide.shape, 1)
    wide = jnp.where(row // KM == column // KM, wide, 0.0)
    return mm(wide, image, NN, high)


def modes_kernel(counts_ref, g_ref, z_hbm, modes_ref, values_ref, z_ref, e_ref, sem):
    groups, freqs, pairs, pts = z_hbm.shape
    fetch = pltpu.make_async_copy(z_hbm, z_ref, sem)
    fetch.start()
    for f in range(freqs):
        top = g_ref[f]
        bottom = exchange(top, True)
        shape = (groups, pairs // 2, 128)
        e = jnp.stack([top.reshape(shape), bottom.reshape(shape)], 1).reshape(128, 128)
        eh, el = split(e)
        e_ref[f, :, :128] = eh
        e_ref[f, :, 128:] = el

    def times_e(basis, f):
        high, low = split(basis)
        r = mm(jnp.concatenate([high, low], 0), e_ref[f])
        return r[:KM, :128] + (r[KM:, :128] + r[:KM, 128:])

    def rows(x, f):
        half = 128 // KM
        return x[f // half][(f % half) * KM : (f % half + 1) * KM]

    def halves(pieces):
        half = 128 // KM
        return [jnp.concatenate(pieces[i : i + half], 0) for i in range(0, freqs, half)]

    image = halves([times_e(g_ref[f, :KM], f) for f in range(freqs)])
    basis = [orthonormal(x) for x in image]
    image = halves([times_e(times_e(rows(basis, f), f), f) for f in range(freqs)])
    basis = [orthonormal(x) for x in image]

    row = lax.broadcasted_iota(jnp.int32, (KM, 128), 0)
    lane = lax.broadcasted_iota(jnp.int32, (KM, 128), 1)
    quotients = jnp.zeros((KM, 128), F32)
    fetch.wait()
    for f in range(freqs):
        b = rows(basis, f)
        high, low = split(b)
        coef = high.astype(F32)
        r = mm(jnp.concatenate([high, low], 0), e_ref[f])
        e_coef = r[:KM, :128] + r[:KM, 128:]
        e_basis = e_coef + r[KM:, :128]
        keep = row[:, :1] < counts_ref[f]
        quotient = jnp.sum(b * e_basis, 1, keepdims=True)
        energy = jnp.sum(coef * e_coef, 1, keepdims=True)
        quotients = jnp.where(lane == f, jnp.where(keep, quotient, 0.0), quotients)
        scale = jnp.where(keep, lax.rsqrt(energy + 1e-06), 0.0)
        both = jnp.concatenate([coef, exchange(coef, False)], 0).astype(BF16)
        field = mm(both, z_ref[:, f].reshape(groups * pairs, pts))
        modes_ref[f] = (field * jnp.concatenate([scale, scale], 0)).astype(BF16)
    padded = jnp.concatenate([quotients] * (128 // KM), 0)
    values_ref[...] = padded.T[:freqs, :KM]


def modes_and_values(counts, g, own):
    groups, freqs, pairs, pts = own.shape
    vmem = pl.BlockSpec(memory_space=pltpu.VMEM)
    return pl.pallas_call(
        modes_kernel,
        in_specs=[
            pl.BlockSpec(memory_space=pltpu.SMEM),
            vmem,
            pl.BlockSpec(memory_space=pl.ANY),
        ],
        out_specs=[vmem, vmem],
        out_shape=[
            jax.ShapeDtypeStruct((freqs, 2 * KM, pts), BF16),
            jax.ShapeDtypeStruct((freqs, KM), F32),
        ],
        scratch_shapes=[
            pltpu.VMEM(own.shape, BF16),
            pltpu.VMEM((freqs, 128, 256), BF16),
            pltpu.SemaphoreType.DMA,
        ],
        compiler_params=pltpu.CompilerParams(vmem_limit_bytes=VMEM_LIMIT),
        name="modes",
    )(counts, g, own)


def local(snapshots, weights, counts):
    blk_dev, steps, pts = snapshots.shape
    groups = lax.axis_size("blk")
    band = counts.shape[0]
    freqs = band * groups
    points_all = pts * lax.axis_size("sp")
    spectra = dft(snapshots, freqs).reshape(groups, band, 2 * blk_dev, pts)
    own = lax.all_to_all(spectra, "blk", split_axis=0, concat_axis=0, tiled=True)
    total = lax.psum(gram(own, weights, points_all), "sp")
    modes, values = modes_and_values(counts, total, own)
    return modes.reshape(band, 2, KM, pts), values


def solution(mesh):
    in_specs = (P("blk", None, "sp"), P("sp"), P("blk"))
    out_specs = (P("blk", None, None, "sp"), P("blk", None))
    return jax.shard_map(local, mesh=mesh, in_specs=in_specs, out_specs=out_specs, check_vma=False)
```

time: 629 us -> 333 us (0.53)
  blocking collectives: 176 us -> 34.3 us
  other arithmetic: 141 us -> 0 us
  matrix products: 20.4 us -> 0 us
  Pallas kernels: 0 us -> 15.7 us
  waiting for transfers between devices: 273 us -> 266 us
    psum x1 -> x0, blocking collectives: 142 us -> none  [local(): energy = lax.psum(local_energy, 'sp') / points_all]
    another operation x19 -> x0, other arithmetic: 135 us -> none  [the longest x9 72.7 us: local(): factor = jnp.linalg.cholesky(cross)]
    dot_general x11 -> x0, matrix products: 19 us -> none  [the longest x1 6.81 us: local(): jnp.einsum('fct,btp->bfcp', table, snapshots, precision=high)]
    pallas_call x0 -> x3, Pallas kernels: none -> 15.7 us  [the longest x1 9.91 us: modes_and_values(): pl.pallas_call(modes_kernel, in_specs=[pl.BlockSpec(memory_space=pltpu.SM...]
    psum x1, waiting for transfers between devices: 273 us -> 266 us  [local(): total = lax.psum(gram(own, weights, points_all), 'sp')]
where the time goes in v1:
time: 333 us
  waiting for transfers between devices  266 us (80%)
  blocking collectives  34.3 us (10%)
  Pallas kernels  15.7 us (5%)
  between operations  14.1 us (4%)
    psum x1, waiting for transfers between devices, local(): total = lax.psum(gram(own, weights, points_all), 'sp')  266 us
    all_to_all x1, blocking collectives, local(): lax.all_to_all(spectra, 'blk', split_axis=0, concat_axis=0, tiled=True)  34.3 us
    pallas_call x1, Pallas kernels, modes_and_values(): pl.pallas_call(modes_kernel, in_specs=[pl.BlockSpec(memory_space=pltpu.SM...  9.91 us
  transfers between devices with their start and end apart: 1, of which 1 were waited for; matrix products, arithmetic and copies ran while one was open for 0% of the time, Pallas kernels for 0%

profile of v1, /device:TPU:8, one launch (start us, length us, event | category | flops | bytes accessed | tf_op | source)
XLA Modules:
  0.0 332.9 jit_solution(7293038454936722522)
XLA Ops:
  7.2 0.0 all-reduce.2.cloned.1.call-start
  7.2 0.0 copy-start.1
  7.2 0.9 copy-done.1
  8.1 0.0 copy-start.2
  8.1 0.9 copy-done.2
  9.0 4.2 %dft.1 = bf16[2048,512]{1,0:T(8,128)(2,1)S(1)} custom-call(bf16[256,256]{1,0:T(8,128)(2,1)S(1)} %copy-done.2, bf16[256,256]{1,0:T(8,128)(2,1)S(1)} %copy-done.1, f32[8,256,512]{2,1,0:T(8,128)} %x_ref.1), custom_call_target="tpu_custom_call" | custom-call | tf_op jit(solution)/shard_map/dft/pallas_call | solution.py:59
  13.2 0.0 copy-start.3
  13.3 34.3 %all_to_all.5.z_ref.z_hbm = bf16[8,16,16,512]{3,2,1,0:T(8,128)(2,1)S(1)} all-to-all(bf16[8,16,16,512]{3,2,1,0:T(8,128)(2,1)S(1)} %bitcast.3), channel_id=1, replica_groups=mesh['blk'=8,'sp'=64] {'blk'}, dimensions={0} | all-to-all | bytes 4194304 | tf_op jit(solution)/shard_map/all_to_all | solution.py:226
  47.6 0.0 copy-start.4
  47.6 0.0 copy-done.3
  47.6 1.6 gram.1
  49.2 0.0 all-reduce.2.cloned.1.call-update
  49.2 265.8 %all-reduce.2.cloned.1.call-done.g_ref = f32[16,64,128]{2,1,0:T(8,128)} async-done(((f32[16,64,128]{2,1,0:T(8,128)}), f32[16,64,128]{2,1,0:T(8,128)}) %all-reduce.2.cloned.1.call-update) | async-done | bytes 524304 | tf_op jit(solution)/shard_map/psum | solution.py:227
  315.0 0.0 copy-done.4
  315.0 0.0 copy-start
  315.0 1.0 copy-done
  316.1 9.9 %modes.1 = (bf16[16,32,512]{2,1,0:T(8,128)(2,1)}, f32[16,16]{1,0:T(8,128)}) custom-call(s32[16]{0:T(128)S(1)} %copy-done.4, f32[16,64,128]{2,1,0:T(8,128)S(1)} %copy-done, bf16[8,16,16,512]{3,2,1,0:T(8,128)(2,1)S(1)} %all_to_all.5.z_ref.z_hbm), custom_call_target="tpu_custom_call" | custom-call | tf_op jit(solution)/shard_map/modes/pallas_call | solution.py:197
Async XLA Ops:
  7.2 307.9 %all-reduce.2.cloned.1.call-start = ((), (), s32[]{:S(2)}) async-start(), calls=%async_computation.1 | async-start | bytes 1048576 | tf_op jit(solution)/shard_map/psum | solution.py:227
  7.2 0.9 copy-start.1
  8.1 0.9 copy-start.2
  13.2 34.3 %copy-start.3 = (f32[512]{0:T(512)S(1)}, f32[512]{0:T(512)}, u32[]{:S(2)}) copy-start(f32[512]{0:T(512)} %param.6) | copy-start | bytes 6148
  47.6 267.5 %copy-start.4 = (s32[16]{0:T(128)S(1)}, s32[16]{0:T(128)}, u32[]{:S(2)}) copy-start(s32[16]{0:T(128)} %counts_ref.1) | copy-start | bytes 196
  315.0 1.0 copy-start
Sparse Core Ops, SparseCore 0:
  49.3 265.6 all-reduce.1

commit v2 on v1

--- a/solution.py
+++ b/solution.py
@@ -82,16 +82,31 @@
     return jnp.where((lane & 8) == 0, up, -down)
 
 
+def places(rows):
+    row = lax.broadcasted_iota(jnp.int32, (rows, 128), 0)
+    lane = lax.broadcasted_iota(jnp.int32, (rows, 128), 1)
+    return row, (lane >> 4) * 8 + (lane & 7), (lane & 8) == 0
+
+
 def gram_kernel(points_all, z_ref, w_ref, out_ref):
     groups, freqs, pairs, pts = z_ref.shape
     weights = w_ref[...]
-    for f in range(freqs):
+    rows = groups * pairs // 2
+    row, block, first = places(rows)
+
+    def one(f):
         z = z_ref[:, f].reshape(groups * pairs, pts)
         zw = (z.astype(F32) * weights).astype(BF16)
         m = mm(zw, z, NT).reshape(groups, 2, pairs // 2, 128)
-        top = m[:, 0].reshape(groups * pairs // 2, 128)
-        bottom = m[:, 1].reshape(groups * pairs // 2, 128)
-        out_ref[f] = (top + exchange(bottom, False)) * (1.0 / points_all)
+        top = m[:, 0].reshape(rows, 128)
+        bottom = m[:, 1].reshape(rows, 128)
+        return (top + exchange(bottom, False)) * (1.0 / points_all)
+
+    for f in range(0, freqs, 2):
+        a, b = one(f), one(f + 1)
+        a = jnp.where(row <= block, a, pltpu.roll(a, 120, 1))
+        b = jnp.where(row <= block, pltpu.roll(b, 8, 1), b)
+        out_ref[f // 2] = jnp.where(first, a, b)
 
 
 def gram(own, weights, points_all):
@@ -100,10 +115,37 @@
         functools.partial(gram_kernel, points_all),
         in_specs=[pl.BlockSpec(memory_space=pltpu.VMEM)] * 2,
         out_specs=pl.BlockSpec(memory_space=pltpu.VMEM),
-        out_shape=jax.ShapeDtypeStruct((freqs, groups * pairs // 2, 128), F32),
+        out_shape=jax.ShapeDtypeStruct((freqs // 2, groups * pairs // 2, 128), F32),
         compiler_params=pltpu.CompilerParams(vmem_limit_bytes=VMEM_LIMIT),
         name="gram",
     )(own, weights.reshape(1, pts))
+
+
+def total_kernel(x_ref, out_ref):
+    total = jnp.sum(x_ref[...], 0)
+    for i in range(out_ref.shape[0]):
+        out_ref[i] = total
+
+
+def total_for(x, copies):
+    return pl.pallas_call(
+        total_kernel,
+        in_specs=[pl.BlockSpec(memory_space=pltpu.VMEM)],
+        out_specs=pl.BlockSpec(memory_space=pltpu.VMEM),
+        out_shape=jax.ShapeDtypeStruct((copies,) + x.shape[1:], F32),
+        compiler_params=pltpu.CompilerParams(vmem_limit_bytes=VMEM_LIMIT),
+        name="total",
+    )(x)
+
+
+def sum_points(packed):
+    nz, nx = lax.axis_size("z"), lax.axis_size("x")
+    pieces = packed.reshape(nz * nx, -1, 128)
+    pieces = lax.all_to_all(pieces, ("z", "x"), split_axis=0, concat_axis=0, tiled=True)
+    mine = total_for(pieces, nz)
+    column = lax.all_to_all(mine, "z", split_axis=0, concat_axis=0, tiled=True)
+    columns = jnp.broadcast_to(column[None], (nx,) + column.shape)
+    return lax.all_to_all(columns, "x", split_axis=0, concat_axis=0, tiled=True)
 
 
 def inverse_factor(cross):
@@ -141,14 +183,34 @@
     groups, freqs, pairs, pts = z_hbm.shape
     fetch = pltpu.make_async_copy(z_hbm, z_ref, sem)
     fetch.start()
-    for f in range(freqs):
-        top = g_ref[f]
-        bottom = exchange(top, True)
-        shape = (groups, pairs // 2, 128)
-        e = jnp.stack([top.reshape(shape), bottom.reshape(shape)], 1).reshape(128, 128)
-        eh, el = split(e)
-        e_ref[f, :, :128] = eh
-        e_ref[f, :, 128:] = el
+    nx, nz = g_ref.shape[:2]
+    row, block, first = places(groups * pairs // 2)
+    upper, lower = row <= block, row > block
+    tall = (groups, pairs // 2, 128)
+
+    def piece(pair):
+        per = groups * pairs // 2 // g_ref.shape[2]
+        return jnp.concatenate([g_ref[i % nx, i // nx] for i in range(pair * per, (pair + 1) * per)], 0)
+
+    starts = []
+    for f in range(0, freqs, 4):
+        q = [piece(f // 2), piece(f // 2 + 1)]
+        t = jnp.stack([q[0].reshape(tall), q[1].reshape(tall)], 1).reshape(128, 128).T
+        t = t.reshape(groups, 2, pairs // 2, 128)
+        t = [t[:, 0].reshape(-1, 128), t[:, 1].reshape(-1, 128)]
+        for i in range(4):
+            p, pt = q[i // 2], t[i % 2]
+            p = pltpu.roll(p, 120, 1) if i % 2 else p
+            pt = pltpu.roll(pt, 120, 1) if i // 2 else pt
+            real = jnp.where(upper, p, pt)
+            imag = jnp.where(lower, -p, jnp.where(row == block, 0.0, pt))
+            top = jnp.where(first, real, pltpu.roll(-imag, 8, 1))
+            bottom = jnp.where(first, imag, pltpu.roll(real, 8, 1))
+            starts.append(top[:KM])
+            e = jnp.stack([top.reshape(tall), bottom.reshape(tall)], 1).reshape(128, 128)
+            eh, el = split(e)
+            e_ref[f + i, :, :128] = eh
+            e_ref[f + i, :, 128:] = el
 
     def times_e(basis, f):
         high, low = split(basis)
@@ -163,7 +225,7 @@
         half = 128 // KM
         return [jnp.concatenate(pieces[i : i + half], 0) for i in range(0, freqs, half)]
 
-    image = halves([times_e(g_ref[f, :KM], f) for f in range(freqs)])
+    image = halves([times_e(starts[f], f) for f in range(freqs)])
     basis = [orthonormal(x) for x in image]
     image = halves([times_e(times_e(rows(basis, f), f), f) for f in range(freqs)])
     basis = [orthonormal(x) for x in image]
@@ -221,15 +283,19 @@
     groups = lax.axis_size("blk")
     band = counts.shape[0]
     freqs = band * groups
-    points_all = pts * lax.axis_size("sp")
+    points_all = pts * lax.axis_size("z") * lax.axis_size("x")
     spectra = dft(snapshots, freqs).reshape(groups, band, 2 * blk_dev, pts)
     own = lax.all_to_all(spectra, "blk", split_axis=0, concat_axis=0, tiled=True)
-    total = lax.psum(gram(own, weights, points_all), "sp")
+    total = sum_points(gram(own, weights, points_all))
     modes, values = modes_and_values(counts, total, own)
     return modes.reshape(band, 2, KM, pts), values
 
 
 def solution(mesh):
-    in_specs = (P("blk", None, "sp"), P("sp"), P("blk"))
-    out_specs = (P("blk", None, None, "sp"), P("blk", None))
+    blk, sp = mesh.devices.shape
+    nx = min(4, sp)
+    mesh = jax.sharding.Mesh(mesh.devices.reshape(blk, sp // nx, nx), ("blk", "z", "x"))
+    points = ("z", "x")
+    in_specs = (P("blk", None, points), P(points), P("blk"))
+    out_specs = (P("blk", None, None, points), P("blk", None))
     return jax.shard_map(local, mesh=mesh, in_specs=in_specs, out_specs=out_specs, check_vma=False)

time: 333 us -> 115 us (0.35)
  the two profiles are of different devices: /device:TPU:8 before, /device:TPU:2 now
where the time goes in v2:
time: 115 us; the launch traced here: 114 us
  blocking collectives  96.5 us (84%)
  Pallas kernels  15.5 us (13%)
  local copies, waits for them, and re-layouts  1.83 us (2%)
    all_to_all x1, blocking collectives, sum_points(): lax.all_to_all(pieces, ('z', 'x'), split_axis=0, concat_axis=0, tiled=True)  39.7 us
    all_to_all x1, blocking collectives, local(): lax.all_to_all(spectra, 'blk', split_axis=0, concat_axis=0, tiled=True)  31.8 us
    all_to_all x1, blocking collectives, sum_points(): column = lax.all_to_all(mine, 'z', split_axis=0, concat_axis=0, tiled=True)  15.8 us
    pallas_call x1, Pallas kernels, modes_and_values(): pl.pallas_call(modes_kernel, in_specs=[pl.BlockSpec(memory_space=pltpu.SM...  10.3 us
    all_to_all x1, blocking collectives, sum_points(): return lax.all_to_all(columns, 'x', split_axis=0, concat_axis=0, tiled=True)  9.19 us
    pallas_call x1, Pallas kernels, dft(): pl.pallas_call(dft_kernel, grid=(pts // wide,), in_specs=[pl.BlockSpec((r...  4.22 us

profile of v2, /device:TPU:2, one launch (start us, length us, event | category | flops | bytes accessed | tf_op | source)
XLA Modules:
  0.0 114.5 jit_solution(538495032510499430)
XLA Ops:
  0.6 0.0 copy-start
  0.6 0.9 copy-done
  1.5 0.0 copy-start.1
  1.5 0.9 copy-done.1
  2.4 4.2 %dft.1 = bf16[2048,512]{1,0:T(8,128)(2,1)S(1)} custom-call(bf16[256,256]{1,0:T(8,128)(2,1)S(1)} %copy-done.1, bf16[256,256]{1,0:T(8,128)(2,1)S(1)} %copy-done, f32[8,256,512]{2,1,0:T(8,128)} %x_ref.1), custom_call_target="tpu_custom_call" | custom-call | tf_op jit(solution)/shard_map/dft/pallas_call | solution.py:59
  6.7 0.0 copy-start.2
  6.7 31.8 %all_to_all.20.z_ref.z_hbm = bf16[8,16,16,512]{3,2,1,0:T(8,128)(2,1)S(1)} all-to-all(bf16[8,16,16,512]{3,2,1,0:T(8,128)(2,1)S(1)} %bitcast.4), channel_id=1, replica_groups=mesh['blk'=8,'z'=16,'x'=4] {'blk'}, dimensions={0} | all-to-all | bytes 4194304 | tf_op jit(solution)/shard_map/all_to_all | solution.py:288
  38.5 0.0 copy-done.2
  38.5 0.0 copy-start.3
  38.5 1.0 gram.1
  39.4 39.7 %all_to_all.21.x_ref = f32[64,8,128]{2,1,0:T(8,128)S(1)} all-to-all(f32[64,8,128]{2,1,0:T(8,128)S(1)} %bitcast.5), channel_id=1, replica_groups=mesh['blk'=8,'z'=16,'x'=4] {'z','x'}, dimensions={0} | all-to-all | bytes 524288 | tf_op jit(solution)/shard_map/all_to_all | solution.py:144
  79.1 0.1 total.1
  79.2 15.8 %all_to_all.22 = f32[16,8,128]{2,1,0:T(8,128)S(1)} all-to-all(f32[16,8,128]{2,1,0:T(8,128)S(1)} %total.1), channel_id=1, replica_groups=mesh['blk'=8,'z'=16,'x'=4] {'z'}, dimensions={0} | all-to-all | bytes 131072 | tf_op jit(solution)/shard_map/all_to_all | solution.py:146
  95.0 9.2 %all_to_all.23.g_ref = f32[4,16,8,128]{3,2,1,0:T(8,128)S(1)} all-to-all(f32[4,16,8,128]{3,2,1,0:T(8,128)S(1)} %broadcast_in_dim.2), channel_id=1, replica_groups=mesh['blk'=8,'z'=16,'x'=4] {'x'}, dimensions={0} | all-to-all | bytes 524288 | tf_op jit(solution)/shard_map/all_to_all | solution.py:148
  104.2 0.0 copy-done.3
  104.2 10.3 %modes.1 = (bf16[16,32,512]{2,1,0:T(8,128)(2,1)}, f32[16,16]{1,0:T(8,128)}) custom-call(s32[16]{0:T(128)S(1)} %copy-done.3, f32[4,16,8,128]{3,2,1,0:T(8,128)S(1)} %all_to_all.23.g_ref, bf16[8,16,16,512]{3,2,1,0:T(8,128)(2,1)S(1)} %all_to_all.20.z_ref.z_hbm), custom_call_target="tpu_custom_call" | custom-call | tf_op jit(solution)/shard_map/modes/pallas_call | solution.py:259
  (1 shorter events, 0.0 us)
Async XLA Ops:
  0.6 0.9 copy-start
  1.5 0.9 copy-start.1
  6.7 31.8 %copy-start.2 = (f32[512]{0:T(512)S(1)}, f32[512]{0:T(512)}, u32[]{:S(2)}) copy-start(f32[512]{0:T(512)} %param.6) | copy-start | bytes 6148
  38.5 65.7 %copy-start.3 = (s32[16]{0:T(128)S(1)}, s32[16]{0:T(128)}, u32[]{:S(2)}) copy-start(s32[16]{0:T(128)} %counts_ref.1) | copy-start | bytes 196

commit v3 on v1

v3 whole, which is shorter than its diff:
```python
import functools

import jax
import jax.numpy as jnp
import ml_dtypes
import numpy as np
from jax import lax
from jax.experimental import pallas as pl
from jax.experimental.pallas import tpu as pltpu
from jax.sharding import PartitionSpec as P

KM = 16
F32 = jnp.float32
BF16 = jnp.bfloat16
NN = (((1,), (0,)), ((), ()))
NT = (((1,), (1,)), ((), ()))
VMEM_LIMIT = 48 * 1024 * 1024


def make_table(freqs, steps):
    times = np.arange(steps)
    phase = (np.arange(freqs)[:, None] * times[None, :]) % steps
    angle = 2.0 * np.pi * phase / steps
    window = np.sqrt(8.0 / (3.0 * steps)) * 0.5 * (1.0 - np.cos(2.0 * np.pi * times / steps))
    table = np.stack([np.cos(angle) * window, np.sin(angle) * window], 1)
    table = table.reshape(2 * freqs, steps).astype(np.float32)
    high = table.astype(ml_dtypes.bfloat16)
    low = (table - high.astype(np.float32)).astype(ml_dtypes.bfloat16)
    return np.concatenate([high, low], 0)


def split(x):
    high = x.astype(BF16)
    return high, (x - high.astype(F32)).astype(BF16)


def mm(a, b, dims=NN, precision=None):
    return lax.dot_general(a, b, dims, preferred_element_type=F32, precision=precision)


def dft_kernel(table_ref, x_ref, out_ref, acc_ref):
    blocks = x_ref.shape[0]
    rows = table_ref.shape[0] // 2
    table = table_ref[...]
    high = table[:rows]
    for b in range(blocks):
        xh, xl = split(x_ref[b])
        both = mm(table, xh)
        acc = both[:rows] + (both[rows:] + mm(high, xl))
        for col in range(0, acc.shape[1], 128):
            acc_ref[col // 128, pl.ds(b, rows, stride=blocks), :] = acc[:, col : col + 128]
    for col in range(0, out_ref.shape[1], 128):
        out_ref[:, col : col + 128] = acc_ref[col // 128].astype(BF16)


def dft(snapshots, freqs):
    blocks, steps, pts = snapshots.shape
    table = make_table(freqs, steps)
    wide = 256
    rows = 2 * freqs
    return pl.pallas_call(
        dft_kernel,
        grid=(pts // wide,),
        in_specs=[
            pl.BlockSpec((2 * rows, steps), lambda i: (0, 0)),
            pl.BlockSpec((blocks, steps, wide), lambda i: (0, 0, i)),
        ],
        out_specs=pl.BlockSpec((rows * blocks, wide), lambda i: (0, i)),
        out_shape=jax.ShapeDtypeStruct((rows * blocks, pts), BF16),
        scratch_shapes=[pltpu.VMEM((wide // 128, rows * blocks, 128), F32)],
        compiler_params=pltpu.CompilerParams(vmem_limit_bytes=VMEM_LIMIT),
        name="dft",
    )(jnp.asarray(table), snapshots)


def exchange(x, sign_first):
    lane = lax.broadcasted_iota(jnp.int32, x.shape, x.ndim - 1)
    last = x.ndim - 1
    up = pltpu.roll(x, 120, last)
    down = pltpu.roll(x, 8, last)
    if sign_first:
        return jnp.where((lane & 8) == 0, -up, down)
    return jnp.where((lane & 8) == 0, up, -down)


def places(rows):
    row = lax.broadcasted_iota(jnp.int32, (rows, 128), 0)
    lane = lax.broadcasted_iota(jnp.int32, (rows, 128), 1)
    return row, (lane >> 4) * 8 + (lane & 7), (lane & 8) == 0


def gram_kernel(points_all, z_ref, w_ref, out_ref):
    groups, freqs, pairs, pts = z_ref.shape
    weights = w_ref[...]
    rows = groups * pairs // 2
    row, block, first = places(rows)
    for f in range(freqs):
        z = z_ref[:, f].reshape(groups * pairs, pts)
        zw = (z.astype(F32) * weights).astype(BF16)
        m = mm(zw, z, NT).reshape(groups, 2, pairs // 2, 128)
        top = m[:, 0].reshape(rows, 128)
        bottom = m[:, 1].reshape(rows, 128)
        g = (top + exchange(bottom, False)) * (1.0 / points_all)
        p = jnp.where(row <= block, g, pltpu.roll(g, 120, 1))
        half = rows // 2
        out_ref[f] = jnp.where(first[:half], p[:half], pltpu.roll(p[half:], 8, 1)).astype(out_ref.dtype)


def call(kernel, out_shape, *args, scratch=(), name):
    vmem = pl.BlockSpec(memory_space=pltpu.VMEM)
    smem = pl.BlockSpec(memory_space=pltpu.SMEM)
    return pl.pallas_call(
        kernel,
        in_specs=[smem if x.dtype == jnp.int32 else vmem for x in args],
        out_specs=jax.tree.map(lambda _: vmem, out_shape),
        out_shape=out_shape,
        scratch_shapes=scratch,
        compiler_params=pltpu.CompilerParams(vmem_limit_bytes=VMEM_LIMIT),
        name=name,
    )(*args)


def total_kernel(x_ref, out_ref):
    total = jnp.sum(x_ref[...].astype(F32), 0)
    for i in range(out_ref.shape[0]):
        out_ref[i] = total


def factor_out(image):
    cross = mm(image, image, NT, lax.Precision.HIGHEST)
    columns = [jnp.broadcast_to(cross[:, k : k + 1], image.shape) for k in range(KM)]
    row = lax.broadcasted_iota(jnp.int32, image.shape, 0)
    pivots = columns[KM - 1]
    for k in range(KM):
        pivot = columns[k][k : k + 1]
        pivots = jnp.where(row == k, pivot, pivots)
        if k < KM - 1:
            factor = jnp.where(row > k, columns[k] * (1.0 / pivot), 0.0)
            for j in range(k + 1, KM):
                columns[j] = columns[j] - factor * columns[j][k : k + 1]
            image = image - factor * image[k : k + 1]
    return image * lax.rsqrt(pivots)


def unpacked(s):
    half = s.shape[0]
    rows = 2 * half
    row, block, first = places(rows)
    p = jnp.concatenate([s, pltpu.roll(s, 120, 1)], 0)
    tall = (rows // 8, 8, 128)
    t = jnp.stack([p.reshape(tall), p.reshape(tall)], 1).reshape(2 * rows, 128).T
    pt = t.reshape(rows // 8, 2, 8, 128)[:, 0].reshape(rows, 128)
    real = jnp.where(row <= block, p, pt)
    imag = jnp.where(row > block, -p, jnp.where(row == block, 0.0, pt))
    top = jnp.where(first, real, pltpu.roll(-imag, 8, 1))
    bottom = jnp.where(first, imag, pltpu.roll(real, 8, 1))
    return jnp.stack([top.reshape(tall), bottom.reshape(tall)], 1).reshape(2 * rows, 128), top


def iterate_kernel(x_ref, out_ref):
    embedded, top = unpacked(jnp.sum(x_ref[...], 0))
    eh, el = split(embedded)
    e = jnp.concatenate([eh, el], 1)

    def times_e(basis):
        high, low = split(basis)
        r = mm(jnp.concatenate([high, low], 0), e)
        return r[:KM, :128], r[KM:, :128] + r[:KM, 128:]

    image = sum(times_e(top[:KM]))
    basis = factor_out(image)
    basis = factor_out(sum(times_e(sum(times_e(basis)))))
    high, low = split(basis)
    r = mm(jnp.concatenate([high, low], 0), e)
    e_coef = r[:KM, :128] + r[:KM, 128:]
    e_basis = e_coef + r[KM:, :128]
    energy = jnp.sum(high.astype(F32) * e_coef, 1, keepdims=True)
    quotient = jnp.sum(basis * e_basis, 1, keepdims=True)
    lane = lax.broadcasted_iota(jnp.int32, (KM, 128), 1)
    rest = jnp.where(lane < 3, lax.rsqrt(jnp.maximum(energy, 0.0) + 1e-06), quotient)
    first = rest.astype(BF16).astype(F32)
    second = (rest - first).astype(BF16).astype(F32)
    third = rest - first - second
    step = jnp.where(lane < 3, lane, lane - 3)
    words = jnp.where(step == 0, first, jnp.where(step == 1, second, third))
    both = jnp.concatenate([high, jnp.where(lane < 6, words, 0.0).astype(BF16)], 0)
    for i in range(out_ref.shape[0]):
        out_ref[i] = both


def modes_kernel(counts_ref, coef_ref, z_ref, modes_ref, values_ref):
    groups, freqs, pairs, pts = z_ref.shape
    row = lax.broadcasted_iota(jnp.int32, (KM, 128), 0)
    lane = lax.broadcasted_iota(jnp.int32, (KM, 128), 1)
    quotients = jnp.zeros((KM, 128), F32)
    for f in range(freqs):
        coef = coef_ref[f, :KM].astype(F32)
        words = coef_ref[f, KM:].astype(F32)
        keep = row[:, :1] < counts_ref[f]
        scale = jnp.where(keep, words[:, 0:1] + words[:, 1:2] + words[:, 2:3], 0.0)
        quotient = jnp.where(keep, words[:, 3:4] + words[:, 4:5] + words[:, 5:6], 0.0)
        quotients = jnp.where(lane == f, quotient, quotients)
        both = jnp.concatenate([coef, exchange(coef, False)], 0).astype(BF16)
        field = mm(both, z_ref[:, f].reshape(groups * pairs, pts))
        modes_ref[f] = (field * jnp.concatenate([scale, scale], 0)).astype(BF16)
    padded = jnp.concatenate([quotients] * (128 // KM), 0)
    values_ref[...] = padded.T[:freqs, :KM]


def local(snapshots, weights, counts):
    blk_dev, steps, pts = snapshots.shape
    groups = lax.axis_size("blk")
    band = counts.shape[0]
    freqs = band * groups
    nz, nx = lax.axis_size("z"), lax.axis_size("x")
    shape = jax.ShapeDtypeStruct
    spectra = dft(snapshots, freqs).reshape(groups, band, 2 * blk_dev, pts)
    own = lax.all_to_all(spectra, "blk", split_axis=0, concat_axis=0, tiled=True)
    half = groups * blk_dev // 2
    packed = call(
        functools.partial(gram_kernel, pts * nz * nx),
        shape((band, half, 128), BF16),
        own,
        weights.reshape(1, pts),
        name="gram",
    )
    parts = lax.all_to_all(packed, "z", split_axis=0, concat_axis=0, tiled=True)
    copies = call(total_kernel, shape((nx, half, 128), F32), parts, name="total")
    columns = lax.all_to_all(copies, "x", split_axis=0, concat_axis=0, tiled=True)
    mine = call(iterate_kernel, shape((nz, 2 * KM, 128), BF16), columns, name="iterate")
    coefs = lax.all_to_all(mine, "z", split_axis=0, concat_axis=0, tiled=True)
    modes, values = call(
        modes_kernel,
        [shape((band, 2 * KM, pts), BF16), shape((band, KM), F32)],
        counts,
        coefs,
        own,
        name="modes",
    )
    return modes.reshape(band, 2, KM, pts), values


def solution(mesh):
    blk, sp = mesh.devices.shape
    nx = min(4, sp)
    mesh = jax.sharding.Mesh(mesh.devices.reshape(blk, sp // nx, nx), ("blk", "z", "x"))
    points = ("z", "x")
    in_specs = (P("blk", None, points), P(points), P("blk"))
    out_specs = (P("blk", None, None, points), P("blk", None))
    return jax.shard_map(local, mesh=mesh, in_specs=in_specs, out_specs=out_specs, check_vma=False)
```

time: 333 us -> 97.8 us (0.29)
  the two profiles are of different devices: /device:TPU:8 before, /device:TPU:32 now
where the time goes in v3:
time: 97.8 us; the launch traced here: 97.6 us
  blocking collectives  87.2 us (89%)
  Pallas kernels  8.75 us (9%)
    all_to_all x1, blocking collectives, local(): lax.all_to_all(spectra, 'blk', split_axis=0, concat_axis=0, tiled=True)  31.8 us
    all_to_all x1, blocking collectives, local(): parts = lax.all_to_all(packed, 'z', split_axis=0, concat_axis=0, tiled=True)  28.7 us
    all_to_all x1, blocking collectives, local(): coefs = lax.all_to_all(mine, 'z', split_axis=0, concat_axis=0, tiled=True)  17 us
    all_to_all x1, blocking collectives, local(): lax.all_to_all(copies, 'x', split_axis=0, concat_axis=0, tiled=True)  9.71 us
    pallas_call x4, Pallas kernels, call(): pl.pallas_call(kernel, in_specs=[smem if x.dtype == jnp.int32 else vmem f...  4.65 us
    pallas_call x1, Pallas kernels, dft(): pl.pallas_call(dft_kernel, grid=(pts // wide,), in_specs=[pl.BlockSpec((2...  4.11 us

profile of v3, /device:TPU:32, one launch (start us, length us, event | category | flops | bytes accessed | tf_op | source)
XLA Modules:
  0.0 97.6 jit_solution(2825946243316385367)
XLA Ops:
  0.6 0.0 copy-start
  0.6 0.9 copy-done
  1.6 4.1 %dft.1 = bf16[2048,512]{1,0:T(8,128)(2,1)S(1)} custom-call(bf16[512,256]{1,0:T(8,128)(2,1)S(1)} %copy-done, f32[8,256,512]{2,1,0:T(8,128)} %x_ref.1), custom_call_target="tpu_custom_call" | custom-call | tf_op jit(solution)/shard_map/dft/pallas_call | solution.py:61
  5.7 0.0 copy-start.1
  5.7 31.8 %all_to_all.20.z_ref = bf16[8,16,16,512]{3,2,1,0:T(8,128)(2,1)S(1)} all-to-all(bf16[8,16,16,512]{3,2,1,0:T(8,128)(2,1)S(1)} %bitcast.3), channel_id=1, replica_groups=mesh['blk'=8,'z'=16,'x'=4] {'blk'}, dimensions={0} | all-to-all | bytes 4194304 | tf_op jit(solution)/shard_map/all_to_all | solution.py:218
  37.5 0.0 copy-start.2
  37.5 0.0 copy-done.1
  37.5 1.0 %gram.1 = bf16[16,32,128]{2,1,0:T(8,128)(2,1)S(1)} custom-call(bf16[8,16,16,512]{3,2,1,0:T(8,128)(2,1)S(1)} %all_to_all.20.z_ref, f32[1,512]{1,0:T(1,128)S(1)} %bitcast.4), custom_call_target="tpu_custom_call" | custom-call | tf_op jit(solution)/shard_map/gram/pallas_call | solution.py:112
  38.5 28.7 %all_to_all.21.x_ref = bf16[16,32,128]{2,1,0:T(8,128)(2,1)S(1)} all-to-all(bf16[16,32,128]{2,1,0:T(8,128)(2,1)S(1)} %gram.1), channel_id=1, replica_groups=mesh['blk'=8,'z'=16,'x'=4] {'z'}, dimensions={0} | all-to-all | bytes 262144 | tf_op jit(solution)/shard_map/all_to_all | solution.py:227
  67.3 9.7 %all_to_all.22.x_ref = f32[4,32,128]{2,1,0:T(8,128)S(1)} all-to-all(f32[4,32,128]{2,1,0:T(8,128)S(1)} %total.1), channel_id=1, replica_groups=mesh['blk'=8,'z'=16,'x'=4] {'x'}, dimensions={0} | all-to-all | bytes 131072 | tf_op jit(solution)/shard_map/all_to_all | solution.py:229
  77.0 1.7 %iterate.1 = bf16[16,32,128]{2,1,0:T(8,128)(2,1)S(1)} custom-call(f32[4,32,128]{2,1,0:T(8,128)S(1)} %all_to_all.22.x_ref), custom_call_target="tpu_custom_call" | custom-call | tf_op jit(solution)/shard_map/iterate/pallas_call | solution.py:112
  78.7 17.0 %all_to_all.23.coef_ref = bf16[16,32,128]{2,1,0:T(8,128)(2,1)S(1)} all-to-all(bf16[16,32,128]{2,1,0:T(8,128)(2,1)S(1)} %iterate.1), channel_id=1, replica_groups=mesh['blk'=8,'z'=16,'x'=4] {'z'}, dimensions={0} | all-to-all | bytes 262144 | tf_op jit(solution)/shard_map/all_to_all | solution.py:231
  95.6 0.0 copy-done.2
  95.6 1.9 %modes.1 = (bf16[16,32,512]{2,1,0:T(8,128)(2,1)}, f32[16,16]{1,0:T(8,128)}) custom-call(s32[16]{0:T(128)S(1)} %copy-done.2, bf16[16,32,128]{2,1,0:T(8,128)(2,1)S(1)} %all_to_all.23.coef_ref, bf16[8,16,16,512]{3,2,1,0:T(8,128)(2,1)S(1)} %all_to_all.20.z_ref), custom_call_target="tpu_custom_call" | custom-call | tf_op jit(solution)/shard_map/modes/pallas_call | solution.py:112
  (1 shorter events, 0.0 us)
Async XLA Ops:
  0.6 1.0 copy-start
  5.7 31.8 %copy-start.1 = (f32[512]{0:T(512)S(1)}, f32[512]{0:T(512)}, u32[]{:S(2)}) copy-start(f32[512]{0:T(512)} %param.5) | copy-start | bytes 6148
  37.5 58.1 %copy-start.2 = (s32[16]{0:T(128)S(1)}, s32[16]{0:T(128)}, u32[]{:S(2)}) copy-start(s32[16]{0:T(128)} %counts_ref.1) | copy-start | bytes 196

commit v4 on v3

--- a/solution.py
+++ b/solution.py
@@ -38,7 +38,7 @@
     return lax.dot_general(a, b, dims, preferred_element_type=F32, precision=precision)
 
 
-def dft_kernel(table_ref, x_ref, out_ref, acc_ref):
+def dft_kernel(table_ref, x_ref, out_ref, spectra_ref):
     blocks = x_ref.shape[0]
     rows = table_ref.shape[0] // 2
     table = table_ref[...]
@@ -46,11 +46,15 @@
     for b in range(blocks):
         xh, xl = split(x_ref[b])
         both = mm(table, xh)
-        acc = both[:rows] + (both[rows:] + mm(high, xl))
-        for col in range(0, acc.shape[1], 128):
-            acc_ref[col // 128, pl.ds(b, rows, stride=blocks), :] = acc[:, col : col + 128]
-    for col in range(0, out_ref.shape[1], 128):
-        out_ref[:, col : col + 128] = acc_ref[col // 128].astype(BF16)
+        spectra_ref[b] = (both[:rows] + (both[rows:] + mm(high, xl))).astype(BF16)
+    size = 256
+    per = size // blocks
+    to = lax.broadcasted_iota(jnp.int32, (size, size), 0)
+    at = lax.broadcasted_iota(jnp.int32, (size, size), 1)
+    order = jnp.where((at % per) * blocks + at // per == to, 1.0, 0.0).astype(BF16)
+    for g in range(rows // per):
+        group = spectra_ref[:, g * per : (g + 1) * per].reshape(size, -1)
+        out_ref[g * size : (g + 1) * size] = mm(order, group).astype(BF16)
 
 
 def dft(snapshots, freqs):
@@ -67,7 +71,7 @@
         ],
         out_specs=pl.BlockSpec((rows * blocks, wide), lambda i: (0, i)),
         out_shape=jax.ShapeDtypeStruct((rows * blocks, pts), BF16),
-        scratch_shapes=[pltpu.VMEM((wide // 128, rows * blocks, 128), F32)],
+        scratch_shapes=[pltpu.VMEM((blocks, rows, wide), BF16)],
         compiler_params=pltpu.CompilerParams(vmem_limit_bytes=VMEM_LIMIT),
         name="dft",
     )(jnp.asarray(table), snapshots)
@@ -121,7 +125,7 @@
 
 
 def total_kernel(x_ref, out_ref):
-    total = jnp.sum(x_ref[...].astype(F32), 0)
+    total = jnp.sum(x_ref[...].astype(F32), 0).astype(out_ref.dtype)
     for i in range(out_ref.shape[0]):
         out_ref[i] = total
 
@@ -157,8 +161,8 @@
     return jnp.stack([top.reshape(tall), bottom.reshape(tall)], 1).reshape(2 * rows, 128), top
 
 
-def iterate_kernel(x_ref, out_ref):
-    embedded, top = unpacked(jnp.sum(x_ref[...], 0))
+def iterate(s):
+    embedded, top = unpacked(s)
     eh, el = split(embedded)
     e = jnp.concatenate([eh, el], 1)
 
@@ -183,9 +187,15 @@
     third = rest - first - second
     step = jnp.where(lane < 3, lane, lane - 3)
     words = jnp.where(step == 0, first, jnp.where(step == 1, second, third))
-    both = jnp.concatenate([high, jnp.where(lane < 6, words, 0.0).astype(BF16)], 0)
-    for i in range(out_ref.shape[0]):
-        out_ref[i] = both
+    return jnp.concatenate([high, jnp.where(lane < 6, words, 0.0).astype(BF16)], 0)
+
+
+def iterate_kernel(x_ref, out_ref):
+    total = jnp.sum(x_ref[...].astype(F32), 0)
+    for f in range(x_ref.shape[1]):
+        result = iterate(total[f])
+        for i in range(out_ref.shape[0]):
+            out_ref[i, f] = result
 
 
 def modes_kernel(counts_ref, coef_ref, z_ref, modes_ref, values_ref):
@@ -212,23 +222,27 @@
     groups = lax.axis_size("blk")
     band = counts.shape[0]
     freqs = band * groups
-    nz, nx = lax.axis_size("z"), lax.axis_size("x")
+    far, near = "far", ("near", "x")
+    nfar, nnear = lax.axis_size(far), lax.axis_size(near)
     shape = jax.ShapeDtypeStruct
     spectra = dft(snapshots, freqs).reshape(groups, band, 2 * blk_dev, pts)
     own = lax.all_to_all(spectra, "blk", split_axis=0, concat_axis=0, tiled=True)
     half = groups * blk_dev // 2
+    each = band // nnear
     packed = call(
-        functools.partial(gram_kernel, pts * nz * nx),
+        functools.partial(gram_kernel, pts * nfar * nnear),
         shape((band, half, 128), BF16),
         own,
         weights.reshape(1, pts),
         name="gram",
     )
-    parts = lax.all_to_all(packed, "z", split_axis=0, concat_axis=0, tiled=True)
-    copies = call(total_kernel, shape((nx, half, 128), F32), parts, name="total")
-    columns = lax.all_to_all(copies, "x", split_axis=0, concat_axis=0, tiled=True)
-    mine = call(iterate_kernel, shape((nz, 2 * KM, 128), BF16), columns, name="iterate")
-    coefs = lax.all_to_all(mine, "z", split_axis=0, concat_axis=0, tiled=True)
+    parts = packed.reshape(nnear, each, half, 128)
+    parts = lax.all_to_all(parts, near, split_axis=0, concat_axis=0, tiled=True)
+    copies = call(total_kernel, shape((nfar, each, half, 128), BF16), parts, name="total")
+    columns = lax.all_to_all(copies, far, split_axis=0, concat_axis=0, tiled=True)
+    mine = call(iterate_kernel, shape((nnear, each, 2 * KM, 128), BF16), columns, name="iterate")
+    coefs = lax.all_to_all(mine, near, split_axis=0, concat_axis=0, tiled=True)
+    coefs = coefs.reshape(band, 2 * KM, 128)
     modes, values = call(
         modes_kernel,
         [shape((band, 2 * KM, pts), BF16), shape((band, KM), F32)],
@@ -242,9 +256,10 @@
 
 def solution(mesh):
     blk, sp = mesh.devices.shape
-    nx = min(4, sp)
-    mesh = jax.sharding.Mesh(mesh.devices.reshape(blk, sp // nx, nx), ("blk", "z", "x"))
-    points = ("z", "x")
+    nx, near = 4, 2
+    devices = mesh.devices.reshape(blk, sp // (near * nx), near, nx)
+    mesh = jax.sharding.Mesh(devices, ("blk", "far", "near", "x"))
+    points = ("far", "near", "x")
     in_specs = (P("blk", None, points), P(points), P("blk"))
     out_specs = (P("blk", None, None, points), P("blk", None))
     return jax.shard_map(local, mesh=mesh, in_specs=in_specs, out_specs=out_specs, check_vma=False)

time: 97.8 us -> 92.6 us (0.947)
  the two profiles are of different devices: /device:TPU:32 before, /device:TPU:2 now
where the time goes in v4:
time: 92.6 us; the launch traced here: 92.3 us
  blocking collectives  80.3 us (87%)
  Pallas kernels  10.4 us (11%)
  local copies, waits for them, and re-layouts  0.96 us (1%)
    all_to_all x1, blocking collectives, local(): lax.all_to_all(spectra, 'blk', split_axis=0, concat_axis=0, tiled=True)  31.8 us
    all_to_all x1, blocking collectives, local(): lax.all_to_all(copies, far, split_axis=0, concat_axis=0, tiled=True)  27.7 us
    all_to_all x1, blocking collectives, local(): parts = lax.all_to_all(parts, near, split_axis=0, concat_axis=0, tiled=True)  11.5 us
    all_to_all x1, blocking collectives, local(): coefs = lax.all_to_all(mine, near, split_axis=0, concat_axis=0, tiled=True)  9.31 us
    pallas_call x4, Pallas kernels, call(): pl.pallas_call(kernel, in_specs=[smem if x.dtype == jnp.int32 else vmem f...  5.9 us
    pallas_call x1, Pallas kernels, dft(): pl.pallas_call(dft_kernel, grid=(pts // wide,), in_specs=[pl.BlockSpec((2...  4.48 us

profile of v4, /device:TPU:2, one launch (start us, length us, event | category | flops | bytes accessed | tf_op | source)
XLA Modules:
  0.0 92.3 jit_solution(10345158024623622096)
XLA Ops:
  0.6 0.0 copy-start
  0.6 0.9 %copy-done = bf16[512,256]{1,0:T(8,128)(2,1)S(1)} copy-done((bf16[512,256]{1,0:T(8,128)(2,1)S(1)}, bf16[512,256]{1,0:T(8,128)(2,1)}, u32[]{:S(2)}) %copy-start) | copy-done | bytes 262168
  1.6 4.5 %dft.1 = bf16[2048,512]{1,0:T(8,128)(2,1)S(1)} custom-call(bf16[512,256]{1,0:T(8,128)(2,1)S(1)} %copy-done, f32[8,256,512]{2,1,0:T(8,128)} %x_ref.1), custom_call_target="tpu_custom_call" | custom-call | tf_op jit(solution)/shard_map/dft/pallas_call | solution.py:65
  6.1 0.0 copy-start.1
  6.1 31.8 %all_to_all.20.z_ref = bf16[8,16,16,512]{3,2,1,0:T(8,128)(2,1)S(1)} all-to-all(bf16[8,16,16,512]{3,2,1,0:T(8,128)(2,1)S(1)} %bitcast.5), channel_id=1, replica_groups=mesh['blk'=8,'far'=8,'near'=2,'x'=4] {'blk'}, dimensions={0} | all-to-all | bytes 4194304 | tf_op jit(solution)/shard_map/all_to_all | solution.py:229
  37.9 0.0 copy-start.2
  37.9 0.0 copy-done.1
  37.9 1.0 %gram.1 = bf16[16,32,128]{2,1,0:T(8,128)(2,1)S(1)} custom-call(bf16[8,16,16,512]{3,2,1,0:T(8,128)(2,1)S(1)} %all_to_all.20.z_ref, f32[1,512]{1,0:T(1,128)S(1)} %bitcast.8), custom_call_target="tpu_custom_call" | custom-call | tf_op jit(solution)/shard_map/gram/pallas_call | solution.py:116
  38.9 11.5 %all_to_all.21.x_ref = bf16[8,2,32,128]{3,2,1,0:T(8,128)(2,1)S(1)} all-to-all(bf16[8,2,32,128]{3,2,1,0:T(8,128)(2,1)S(1)} %bitcast.7), channel_id=1, replica_groups=mesh['blk'=8,'far'=8,'near'=2,'x'=4] {'near','x'}, dimensions={0} | all-to-all | bytes 262144 | tf_op jit(solution)/shard_map/all_to_all | solution.py:240
  50.5 27.7 %all_to_all.22.x_ref = bf16[8,2,32,128]{3,2,1,0:T(8,128)(2,1)S(1)} all-to-all(bf16[8,2,32,128]{3,2,1,0:T(8,128)(2,1)S(1)} %total.1), channel_id=1, replica_groups=mesh['blk'=8,'far'=8,'near'=2,'x'=4] {'far'}, dimensions={0} | all-to-all | bytes 262144 | tf_op jit(solution)/shard_map/all_to_all | solution.py:242
  78.1 2.9 %iterate.1 = bf16[8,2,32,128]{3,2,1,0:T(8,128)(2,1)S(1)} custom-call(bf16[8,2,32,128]{3,2,1,0:T(8,128)(2,1)S(1)} %all_to_all.22.x_ref), custom_call_target="tpu_custom_call" | custom-call | tf_op jit(solution)/shard_map/iterate/pallas_call | solution.py:116
  81.1 9.3 %all_to_all.23 = bf16[8,2,32,128]{3,2,1,0:T(8,128)(2,1)S(1)} all-to-all(bf16[8,2,32,128]{3,2,1,0:T(8,128)(2,1)S(1)} %iterate.1), channel_id=1, replica_groups=mesh['blk'=8,'far'=8,'near'=2,'x'=4] {'near','x'}, dimensions={0} | all-to-all | bytes 262144 | tf_op jit(solution)/shard_map/all_to_all | solution.py:244
  90.4 0.0 copy-done.2
  90.4 1.9 %modes.1 = (bf16[16,32,512]{2,1,0:T(8,128)(2,1)}, f32[16,16]{1,0:T(8,128)}) custom-call(s32[16]{0:T(128)S(1)} %copy-done.2, bf16[16,32,128]{2,1,0:T(8,128)(2,1)S(1)} %bitcast.6, bf16[8,16,16,512]{3,2,1,0:T(8,128)(2,1)S(1)} %all_to_all.20.z_ref), custom_call_target="tpu_custom_call" | custom-call | tf_op jit(solution)/shard_map/modes/pallas_call | solution.py:116
  (1 shorter events, 0.0 us)
Async XLA Ops:
  0.6 1.0 %copy-start = (bf16[512,256]{1,0:T(8,128)(2,1)S(1)}, bf16[512,256]{1,0:T(8,128)(2,1)}, u32[]{:S(2)}) copy-start(bf16[512,256]{1,0:T(8,128)(2,1)} %constant.2.clone.table_ref) | copy-start | bytes 786436
  6.1 31.8 %copy-start.1 = (f32[512]{0:T(512)S(1)}, f32[512]{0:T(512)}, u32[]{:S(2)}) copy-start(f32[512]{0:T(512)} %param.5) | copy-start | bytes 6148
  37.9 52.5 %copy-start.2 = (s32[16]{0:T(128)S(1)}, s32[16]{0:T(128)}, u32[]{:S(2)}) copy-start(s32[16]{0:T(128)} %counts_ref.1) | copy-start | bytes 196

commit v5 on v3

v5 whole, which is shorter than its diff:
```python
import functools

import jax
import jax.numpy as jnp
import ml_dtypes
import numpy as np
from jax import lax
from jax.experimental import pallas as pl
from jax.experimental.pallas import tpu as pltpu
from jax.sharding import PartitionSpec as P

KM = 16
F32 = jnp.float32
BF16 = jnp.bfloat16
NN = (((1,), (0,)), ((), ()))
NT = (((1,), (1,)), ((), ()))
GROUPS = 8
PARTS = 2
VMEM_LIMIT = 48 * 1024 * 1024


def make_table(freqs, steps):
    times = np.arange(steps)
    phase = (np.arange(freqs)[:, None] * times[None, :]) % steps
    angle = 2.0 * np.pi * phase / steps
    window = np.sqrt(8.0 / (3.0 * steps)) * 0.5 * (1.0 - np.cos(2.0 * np.pi * times / steps))
    table = np.stack([np.cos(angle) * window, np.sin(angle) * window], 1)
    table = table.reshape(2 * freqs, steps).astype(np.float32)
    high = table.astype(ml_dtypes.bfloat16)
    low = (table - high.astype(np.float32)).astype(ml_dtypes.bfloat16)
    return np.concatenate([high, low], 0)


def split(x):
    high = x.astype(BF16)
    return high, (x - high.astype(F32)).astype(BF16)


def mm(a, b, dims=NN, precision=None):
    return lax.dot_general(a, b, dims, preferred_element_type=F32, precision=precision)


def dft_kernel(ids_ref, table_ref, x_ref, *refs):
    out_refs, acc_ref = refs[:-1], refs[-1]
    blocks = x_ref.shape[0]
    rows = table_ref.shape[0] // 2
    high, low = table_ref[:rows], table_ref[rows:]
    table = jnp.concatenate([high, low, high], 1)
    for b in range(blocks):
        xh, xl = split(x_ref[b])
        acc = mm(table, jnp.concatenate([xh, xh, xl], 0))
        for col in range(0, acc.shape[1], 128):
            acc_ref[col // 128, pl.ds(b, rows, stride=blocks), :] = acc[:, col : col + 128]
    for mask, out_ref in enumerate(out_refs):
        size = out_ref.shape[0]
        start = pl.multiple_of((ids_ref[0] ^ mask) * size, size)
        for col in range(0, out_ref.shape[1], 128):
            out_ref[:, col : col + 128] = acc_ref[col // 128, pl.ds(start, size), :].astype(BF16)


def dft(ids, snapshots, groups, freqs, part, parts):
    blocks, steps, pts = snapshots.shape
    table = make_table(freqs, steps)
    wide = pts // parts
    rows = 2 * freqs
    size = rows * blocks // groups
    return pl.pallas_call(
        dft_kernel,
        grid=(1,),
        in_specs=[
            pl.BlockSpec(memory_space=pltpu.SMEM),
            pl.BlockSpec((2 * rows, steps), lambda i: (0, 0)),
            pl.BlockSpec((blocks, steps, wide), lambda i: (0, 0, part)),
        ],
        out_specs=[pl.BlockSpec((size, wide), lambda i: (0, 0))] * groups,
        out_shape=[jax.ShapeDtypeStruct((size, wide), BF16)] * groups,
        scratch_shapes=[pltpu.VMEM((wide // 128, rows * blocks, 128), F32)],
        compiler_params=pltpu.CompilerParams(vmem_limit_bytes=VMEM_LIMIT),
        cost_estimate=pl.CostEstimate(
            flops=6 * rows * steps * blocks * wide, bytes_accessed=4 * 1024 * 1024, transcendentals=0
        ),
        name="dft",
    )(ids, jnp.asarray(table), snapshots)


def exchange(x, sign_first):
    lane = lax.broadcasted_iota(jnp.int32, x.shape, x.ndim - 1)
    last = x.ndim - 1
    up = pltpu.roll(x, 120, last)
    down = pltpu.roll(x, 8, last)
    if sign_first:
        return jnp.where((lane & 8) == 0, -up, down)
    return jnp.where((lane & 8) == 0, up, -down)


def places(rows):
    row = lax.broadcasted_iota(jnp.int32, (rows, 128), 0)
    lane = lax.broadcasted_iota(jnp.int32, (rows, 128), 1)
    return row, (lane >> 4) * 8 + (lane & 7), (lane & 8) == 0


def rows_of(z_refs, parts, f, freqs):
    groups = len(z_refs) // parts
    pairs = z_refs[0].shape[0] // freqs
    start = f * pairs if isinstance(f, int) else pl.multiple_of(f * pairs, pairs)
    pieces = []
    for part in range(parts):
        refs = z_refs[part * groups : (part + 1) * groups]
        pieces.append(jnp.concatenate([ref[pl.ds(start, pairs)] for ref in refs], 0))
    return jnp.concatenate(pieces, 1)


def gram_kernel(points_all, parts, ids_ref, w_ref, *refs):
    nnear = len(refs) - 1 - parts * GROUPS
    z_refs, out_refs, all_ref = refs[: parts * GROUPS], refs[-1 - nnear : -1], refs[-1]
    freqs = all_ref.shape[0]
    weights = w_ref[...]
    rows = 8 * GROUPS
    row, block, first = places(rows)
    for f in range(freqs):
        z = rows_of(z_refs, parts, f, freqs)
        zw = (z.astype(F32) * weights).astype(BF16)
        m = mm(zw, z, NT).reshape(GROUPS, 2, 8, 128)
        top = m[:, 0].reshape(rows, 128)
        bottom = m[:, 1].reshape(rows, 128)
        g = (top + exchange(bottom, False)) * (1.0 / points_all)
        p = jnp.where(row <= block, g, pltpu.roll(g, 120, 1))
        half = rows // 2
        all_ref[f] = jnp.where(first[:half], p[:half], pltpu.roll(p[half:], 8, 1)).astype(BF16)
    each = freqs // nnear
    for mask, out_ref in enumerate(out_refs):
        out_ref[...] = all_ref[pl.ds((ids_ref[1] ^ mask) * each, each)]


def call(kernel, out_shape, *args, scratch=(), name):
    vmem = pl.BlockSpec(memory_space=pltpu.VMEM)
    smem = pl.BlockSpec(memory_space=pltpu.SMEM)
    return pl.pallas_call(
        kernel,
        in_specs=[smem if x.dtype == jnp.int32 else vmem for x in args],
        out_specs=jax.tree.map(lambda _: vmem, out_shape),
        out_shape=out_shape,
        scratch_shapes=scratch,
        compiler_params=pltpu.CompilerParams(vmem_limit_bytes=VMEM_LIMIT),
        name=name,
    )(*args)


def total_kernel(*refs):
    total = refs[0][...].astype(F32)
    for ref in refs[1:-1]:
        total = total + ref[...].astype(F32)
    refs[-1][...] = total.astype(BF16)


def factor_out(images):
    images = list(images)
    every = range(len(images))
    cross = [mm(x, x, NT, lax.Precision.HIGHEST) for x in images]
    columns = [[jnp.broadcast_to(c[:, k : k + 1], (KM, 128)) for k in range(KM)] for c in cross]
    row = lax.broadcasted_iota(jnp.int32, (KM, 128), 0)
    pivots = [columns[f][KM - 1] for f in every]
    for k in range(KM):
        for f in every:
            pivot = columns[f][k][k : k + 1]
            pivots[f] = jnp.where(row == k, pivot, pivots[f])
            if k < KM - 1:
                factor = jnp.where(row > k, columns[f][k] * (1.0 / pivot), 0.0)
                for j in range(k + 1, KM):
                    columns[f][j] = columns[f][j] - factor * columns[f][j][k : k + 1]
                images[f] = images[f] - factor * images[f][k : k + 1]
    return [x * lax.rsqrt(p) for x, p in zip(images, pivots)]


def unpacked(s):
    half = s.shape[0]
    rows = 2 * half
    row, block, first = places(rows)
    p = jnp.concatenate([s, pltpu.roll(s, 120, 1)], 0)
    tall = (rows // 8, 8, 128)
    t = jnp.stack([p.reshape(tall), p.reshape(tall)], 1).reshape(2 * rows, 128).T
    pt = t.reshape(rows // 8, 2, 8, 128)[:, 0].reshape(rows, 128)
    real = jnp.where(row <= block, p, pt)
    imag = jnp.where(row > block, -p, jnp.where(row == block, 0.0, pt))
    top = jnp.where(first, real, pltpu.roll(-imag, 8, 1))
    bottom = jnp.where(first, imag, pltpu.roll(real, 8, 1))
    return jnp.stack([top.reshape(tall), bottom.reshape(tall)], 1).reshape(2 * rows, 128), top


def iterate_kernel(ids_ref, *refs):
    x_refs, out_ref, x_ref, top_ref = refs[:-3], refs[-3], refs[-2], refs[-1]
    for mask, ref in enumerate(x_refs):
        x_ref[ids_ref[2] ^ mask] = ref[...].astype(F32)
    total = jnp.sum(x_ref[...], 0)
    every = range(total.shape[0])
    e, starts = [], []
    for f in every:
        embedded, top = unpacked(total[f])
        e.append(jnp.concatenate(split(embedded), 1))
        top_ref[f] = top
    for f in every:
        at = [pl.multiple_of((ids_ref[0] ^ s) * 8, 8) for s in range(KM // 8)]
        starts.append(jnp.concatenate([top_ref[f, pl.ds(i, 8), :] for i in at], 0))

    def products(basis):
        r = [mm(jnp.concatenate(split(x), 0), e[f]) for f, x in enumerate(basis)]
        return [(x[:KM, :128], x[KM:, :128], x[:KM, 128:]) for x in r]

    def times_e(basis):
        return [a + (b + c) for a, b, c in products(basis)]

    basis = factor_out(times_e(starts))
    basis = factor_out(times_e(times_e(basis)))
    lane = lax.broadcasted_iota(jnp.int32, (KM, 128), 1)
    for f, (a, b, c) in enumerate(products(basis)):
        high = basis[f].astype(BF16)
        energy = jnp.sum(high.astype(F32) * (a + c), 1, keepdims=True)
        quotient = jnp.sum(basis[f] * (a + (b + c)), 1, keepdims=True)
        rest = jnp.where(lane < 3, lax.rsqrt(jnp.maximum(energy, 0.0) + 1e-06), quotient)
        first = rest.astype(BF16).astype(F32)
        second = (rest - first).astype(BF16).astype(F32)
        third = rest - first - second
        step = jnp.where(lane < 3, lane, lane - 3)
        words = jnp.where(step == 0, first, jnp.where(step == 1, second, third))
        out_ref[f] = jnp.concatenate([high, jnp.where(lane < 6, words, 0.0).astype(BF16)], 0)


def modes_kernel(parts, ids_ref, counts_ref, *refs):
    modes_ref, values_ref = refs[-2:]
    z_refs, coef_refs = refs[: parts * GROUPS], refs[parts * GROUPS : -2]
    freqs = counts_ref.shape[0]
    each = coef_refs[0].shape[0]
    row = lax.broadcasted_iota(jnp.int32, (KM, 128), 0)
    lane = lax.broadcasted_iota(jnp.int32, (KM, 128), 1)
    quotients = jnp.zeros((KM, 128), F32)
    for mask, ref in enumerate(coef_refs):
        for i in range(each):
            f = (ids_ref[1] ^ mask) * each + i
            coef = ref[i, :KM].astype(F32)
            words = ref[i, KM:].astype(F32)
            keep = row[:, :1] < counts_ref[f]
            scale = jnp.where(keep, words[:, 0:1] + words[:, 1:2] + words[:, 2:3], 0.0)
            quotient = jnp.where(keep, words[:, 3:4] + words[:, 4:5] + words[:, 5:6], 0.0)
            quotients = jnp.where(lane == f, quotient, quotients)
            both = jnp.concatenate([coef, exchange(coef, False)], 0).astype(BF16)
            field = mm(both, rows_of(z_refs, parts, f, freqs))
            modes_ref[f] = (field * jnp.concatenate([scale, scale], 0)).astype(BF16)
    padded = jnp.concatenate([quotients] * (128 // KM), 0)
    values_ref[...] = padded.T[:freqs, :KM]


def swap(pieces, axis):
    size = lax.axis_size(axis)
    moved = [lax.ppermute(pieces[m], axis, [(i, i ^ m) for i in range(size)]) for m in range(1, size)]
    return [pieces[0]] + moved


def local(snapshots, weights, counts):
    pts = snapshots.shape[2]
    groups = lax.axis_size("blk")
    band = counts.shape[0]
    far, near = "far", ("near", "x")
    nfar, nnear = lax.axis_size(far), lax.axis_size(near)
    ids = jnp.stack([lax.axis_index("blk"), lax.axis_index(near), lax.axis_index(far)]).astype(jnp.int32)
    shape = jax.ShapeDtypeStruct
    each, half = band // nnear, 4 * GROUPS
    own = []
    for part in range(PARTS):
        own += swap(dft(ids, snapshots, groups, band * groups, part, PARTS), "blk")
    packed = call(
        functools.partial(gram_kernel, pts * nfar * nnear, PARTS),
        [shape((each, half, 128), BF16)] * nnear,
        ids,
        weights.reshape(1, pts),
        *own,
        scratch=[pltpu.VMEM((band, half, 128), BF16)],
        name="gram",
    )
    mine = call(total_kernel, shape((each, half, 128), BF16), *swap(packed, near), name="total")
    coefs = call(
        iterate_kernel,
        shape((each, 2 * KM, 128), BF16),
        ids,
        *swap([mine] * nfar, far),
        scratch=[pltpu.VMEM((nfar, each, half, 128), F32), pltpu.VMEM((each, 2 * half, 128), F32)],
        name="iterate",
    )
    modes, values = call(
        functools.partial(modes_kernel, PARTS),
        [shape((band, 2 * KM, pts), BF16), shape((band, KM), F32)],
        ids,
        counts,
        *own,
        *swap([coefs] * nnear, near),
        name="modes",
    )
    return modes.reshape(band, 2, KM, pts), values


def solution(mesh):
    blk, sp = mesh.devices.shape
    nx, near = 4, 2
    devices = mesh.devices.reshape(blk, sp // (near * nx), near, nx)
    mesh = jax.sharding.Mesh(devices, ("blk", "far", "near", "x"))
    points = ("far", "near", "x")
    in_specs = (P("blk", None, points), P(points), P("blk"))
    out_specs = (P("blk", None, None, points), P("blk", None))
    return jax.shard_map(local, mesh=mesh, in_specs=in_specs, out_specs=out_specs, check_vma=False)
```

time: 97.8 us -> 166 us (1.70)
  the two profiles are of different devices: /device:TPU:32 before, /device:TPU:2 now
where the time goes in v5:
time: 166 us; the launch traced here: 165 us
  starting transfers between devices  135 us (81%)
  waiting for transfers between devices  15.8 us (10%)
  Pallas kernels  9.61 us (6%)
  local copies, waits for them, and re-layouts  3.15 us (2%)
    ppermute x35, starting transfers between devices, swap(): lax.ppermute(pieces[m], axis, [(i, i ^ m) for i in range(size)])  135 us
    ppermute x35, waiting for transfers between devices, swap(): lax.ppermute(pieces[m], axis, [(i, i ^ m) for i in range(size)])  15.8 us
    pallas_call x4, Pallas kernels, call(): pl.pallas_call(kernel, in_specs=[smem if x.dtype == jnp.int32 else vmem f...  5.89 us
    pallas_call x2, Pallas kernels, dft(): pl.pallas_call(dft_kernel, grid=(1,), in_specs=[pl.BlockSpec(memory_space...  3.72 us
  transfers between devices with their start and end apart: 35, of which 6 were waited for; matrix products, arithmetic and copies ran while one was open for 0% of the time, Pallas kernels for 1%

profile of v5, /device:TPU:2, one launch (start us, length us, event | category | flops | bytes accessed | tf_op | source)
XLA Modules:
  0.0 165.2 jit_solution(5025850854657465433)
XLA Ops:
  7.7 3.5 %collective-permute-start.8 = (bf16[256,256]{1,0:T(8,128)(2,1)S(1)}, bf16[256,256]{1,0:T(8,128)(2,1)S(1)}, u32[]{:S(2)}, u32[]{:S(2)}) collective-permute-start(bf16[256,256]{1,0:T(8,128)(2,1)S(1)} %get-tuple-element.38), channel_id=1, source_target_pairs={{0,128},{64,192},{128,0},{192,64},{256,384},{320,448},{384,256},{4... | collective-permute-start | bytes 393224 | tf_op jit(solution)/shard_map/ppermute | solution.py:254
  13.3 5.1 %collective-permute-start.10 = (bf16[256,256]{1,0:T(8,128)(2,1)S(1)}, bf16[256,256]{1,0:T(8,128)(2,1)S(1)}, u32[]{:S(2)}, u32[]{:S(2)}) collective-permute-start(bf16[256,256]{1,0:T(8,128)(2,1)S(1)} %get-tuple-element.40), channel_id=1, source_target_pairs={{0,256},{64,320},{128,384},{192,448},{256,0},{320,64},{384,128},{4... | collective-permute-start | bytes 393224 | tf_op jit(solution)/shard_map/ppermute | solution.py:254
  22.3 4.9 %collective-permute-start.12 = (bf16[256,256]{1,0:T(8,128)(2,1)S(1)}, bf16[256,256]{1,0:T(8,128)(2,1)S(1)}, u32[]{:S(2)}, u32[]{:S(2)}) collective-permute-start(bf16[256,256]{1,0:T(8,128)(2,1)S(1)} %get-tuple-element.42), channel_id=1, source_target_pairs={{0,384},{64,448},{128,256},{192,320},{256,128},{320,192},{384,0},{... | collective-permute-start | bytes 393224 | tf_op jit(solution)/shard_map/ppermute | solution.py:254
  33.6 3.2 %collective-permute-start.2 = (bf16[256,256]{1,0:T(8,128)(2,1)S(1)}, bf16[256,256]{1,0:T(8,128)(2,1)S(1)}, u32[]{:S(2)}, u32[]{:S(2)}) collective-permute-start(bf16[256,256]{1,0:T(8,128)(2,1)S(1)} %get-tuple-element.31), channel_id=1, source_target_pairs={{0,192},{64,128},{128,64},{192,0},{256,448},{320,384},{384,320},{4... | collective-permute-start | bytes 393224 | tf_op jit(solution)/shard_map/ppermute | solution.py:254
  36.8 4.8 %collective-permute-start.3 = (bf16[256,256]{1,0:T(8,128)(2,1)S(1)}, bf16[256,256]{1,0:T(8,128)(2,1)S(1)}, u32[]{:S(2)}, u32[]{:S(2)}) collective-permute-start(bf16[256,256]{1,0:T(8,128)(2,1)S(1)} %get-tuple-element.32), channel_id=1, source_target_pairs={{0,256},{64,320},{128,384},{192,448},{256,0},{320,64},{384,128},{4... | collective-permute-start | bytes 393224 | tf_op jit(solution)/shard_map/ppermute | solution.py:254
  44.1 4.9 %collective-permute-start.5 = (bf16[256,256]{1,0:T(8,128)(2,1)S(1)}, bf16[256,256]{1,0:T(8,128)(2,1)S(1)}, u32[]{:S(2)}, u32[]{:S(2)}) collective-permute-start(bf16[256,256]{1,0:T(8,128)(2,1)S(1)} %get-tuple-element.34), channel_id=1, source_target_pairs={{0,384},{64,448},{128,256},{192,320},{256,128},{320,192},{384,0},{... | collective-permute-start | bytes 393224 | tf_op jit(solution)/shard_map/ppermute | solution.py:254
  50.9 2.7 %collective-permute-done.5.refs_6_ = bf16[256,256]{1,0:T(8,128)(2,1)S(1)} collective-permute-done((bf16[256,256]{1,0:T(8,128)(2,1)S(1)}, bf16[256,256]{1,0:T(8,128)(2,1)S(1)}, u32[]{:S(2)}, u32[]{:S(2)}) %collective-permute-start.5) | collective-permute-done | bytes 131104 | tf_op jit(solution)/shard_map/ppermute | solution.py:254
  53.6 4.2 %collective-permute-done.6.refs_7_ = bf16[256,256]{1,0:T(8,128)(2,1)S(1)} collective-permute-done((bf16[256,256]{1,0:T(8,128)(2,1)S(1)}, bf16[256,256]{1,0:T(8,128)(2,1)S(1)}, u32[]{:S(2)}, u32[]{:S(2)}) %collective-permute-start.6) | collective-permute-done | bytes 131104 | tf_op jit(solution)/shard_map/ppermute | solution.py:254
  59.3 5.2 %collective-permute-start.14 = (bf16[2,32,128]{2,1,0:T(8,128)(2,1)S(1)}, bf16[2,32,128]{2,1,0:T(8,128)(2,1)S(1)}, u32[]{:S(2)}, u32[]{:S(2)}) collective-permute-start(bf16[2,32,128]{2,1,0:T(8,128)(2,1)S(1)} %get-tuple-element.45), channel_id=1, source_target_pairs={{0,1},{1,0},{2,3},{3,2},{4,5},{5,4},{6,7},{7,6},{8,9},{9,8},{10,11... | collective-permute-start | bytes 49160 | tf_op jit(solution)/shard_map/ppermute | solution.py:254
  66.4 3.4 %collective-permute-start.16 = (bf16[2,32,128]{2,1,0:T(8,128)(2,1)S(1)}, bf16[2,32,128]{2,1,0:T(8,128)(2,1)S(1)}, u32[]{:S(2)}, u32[]{:S(2)}) collective-permute-start(bf16[2,32,128]{2,1,0:T(8,128)(2,1)S(1)} %get-tuple-element.47), channel_id=1, source_target_pairs={{0,3},{1,2},{2,1},{3,0},{4,7},{5,6},{6,5},{7,4},{8,11},{9,10},{10,... | collective-permute-start | bytes 49160 | tf_op jit(solution)/shard_map/ppermute | solution.py:254
  72.3 5.9 %collective-permute-start.18 = (bf16[2,32,128]{2,1,0:T(8,128)(2,1)S(1)}, bf16[2,32,128]{2,1,0:T(8,128)(2,1)S(1)}, u32[]{:S(2)}, u32[]{:S(2)}) collective-permute-start(bf16[2,32,128]{2,1,0:T(8,128)(2,1)S(1)} %get-tuple-element.49), channel_id=1, source_target_pairs={{0,5},{1,4},{2,7},{3,6},{4,1},{5,0},{6,3},{7,2},{8,13},{9,12},{10,... | collective-permute-start | bytes 49160 | tf_op jit(solution)/shard_map/ppermute | solution.py:254
  80.2 3.1 %collective-permute-start.20 = (bf16[2,32,128]{2,1,0:T(8,128)(2,1)S(1)}, bf16[2,32,128]{2,1,0:T(8,128)(2,1)S(1)}, u32[]{:S(2)}, u32[]{:S(2)}) collective-permute-start(bf16[2,32,128]{2,1,0:T(8,128)(2,1)S(1)} %get-tuple-element.51), channel_id=1, source_target_pairs={{0,7},{1,6},{2,5},{3,4},{4,3},{5,2},{6,1},{7,0},{8,15},{9,14},{10,... | collective-permute-start | bytes 49160 | tf_op jit(solution)/shard_map/ppermute | solution.py:254
  83.3 3.0 %collective-permute-done.19.refs_6_ = bf16[2,32,128]{2,1,0:T(8,128)(2,1)S(1)} collective-permute-done((bf16[2,32,128]{2,1,0:T(8,128)(2,1)S(1)}, bf16[2,32,128]{2,1,0:T(8,128)(2,1)S(1)}, u32[]{:S(2)}, u32[]{:S(2)}) %collective-permute-start.19) | collective-permute-done | bytes 16416 | tf_op jit(solution)/shard_map/ppermute | solution.py:254
  86.8 10.8 %collective-permute-start.27 = (bf16[2,32,128]{2,1,0:T(8,128)(2,1)S(1)}, bf16[2,32,128]{2,1,0:T(8,128)(2,1)S(1)}, u32[]{:S(2)}, u32[]{:S(2)}) collective-permute-start(bf16[2,32,128]{2,1,0:T(8,128)(2,1)S(1)} %total.1.refs_0_), channel_id=1, source_target_pairs={{0,56},{8,48},{16,40},{24,32},{32,24},{40,16},{48,8},{56,0},{1,57}... | collective-permute-start | bytes 49160 | tf_op jit(solution)/shard_map/ppermute | solution.py:254
  97.5 2.8 %collective-permute-start.26 = (bf16[2,32,128]{2,1,0:T(8,128)(2,1)S(1)}, bf16[2,32,128]{2,1,0:T(8,128)(2,1)S(1)}, u32[]{:S(2)}, u32[]{:S(2)}) collective-permute-start(bf16[2,32,128]{2,1,0:T(8,128)(2,1)S(1)} %total.1.refs_0_), channel_id=1, source_target_pairs={{0,48},{8,56},{16,32},{24,40},{32,16},{40,24},{48,0},{56,8},{1,49}... | collective-permute-start | bytes 49160 | tf_op jit(solution)/shard_map/ppermute | solution.py:254
  100.4 9.0 %collective-permute-start.25 = (bf16[2,32,128]{2,1,0:T(8,128)(2,1)S(1)}, bf16[2,32,128]{2,1,0:T(8,128)(2,1)S(1)}, u32[]{:S(2)}, u32[]{:S(2)}) collective-permute-start(bf16[2,32,128]{2,1,0:T(8,128)(2,1)S(1)} %total.1.refs_0_), channel_id=1, source_target_pairs={{0,40},{8,32},{16,56},{24,48},{32,8},{40,0},{48,24},{56,16},{1,41}... | collective-permute-start | bytes 49160 | tf_op jit(solution)/shard_map/ppermute | solution.py:254
  109.4 5.6 %collective-permute-start.24 = (bf16[2,32,128]{2,1,0:T(8,128)(2,1)S(1)}, bf16[2,32,128]{2,1,0:T(8,128)(2,1)S(1)}, u32[]{:S(2)}, u32[]{:S(2)}) collective-permute-start(bf16[2,32,128]{2,1,0:T(8,128)(2,1)S(1)} %total.1.refs_0_), channel_id=1, source_target_pairs={{0,32},{8,40},{16,48},{24,56},{32,0},{40,8},{48,16},{56,24},{1,33}... | collective-permute-start | bytes 49160 | tf_op jit(solution)/shard_map/ppermute | solution.py:254
  115.0 6.3 %collective-permute-start.23 = (bf16[2,32,128]{2,1,0:T(8,128)(2,1)S(1)}, bf16[2,32,128]{2,1,0:T(8,128)(2,1)S(1)}, u32[]{:S(2)}, u32[]{:S(2)}) collective-permute-start(bf16[2,32,128]{2,1,0:T(8,128)(2,1)S(1)} %total.1.refs_0_), channel_id=1, source_target_pairs={{0,24},{8,16},{16,8},{24,0},{32,56},{40,48},{48,40},{56,32},{1,25}... | collective-permute-start | bytes 49160 | tf_op jit(solution)/shard_map/ppermute | solution.py:254
  123.3 5.8 %collective-permute-start.21 = (bf16[2,32,128]{2,1,0:T(8,128)(2,1)S(1)}, bf16[2,32,128]{2,1,0:T(8,128)(2,1)S(1)}, u32[]{:S(2)}, u32[]{:S(2)}) collective-permute-start(bf16[2,32,128]{2,1,0:T(8,128)(2,1)S(1)} %total.1.refs_0_), channel_id=1, source_target_pairs={{0,8},{8,0},{16,24},{24,16},{32,40},{40,32},{48,56},{56,48},{1,9},... | collective-permute-start | bytes 49160 | tf_op jit(solution)/shard_map/ppermute | solution.py:254
  133.3 2.9 %collective-permute-start.34 = (bf16[2,32,128]{2,1,0:T(8,128)(2,1)S(1)}, bf16[2,32,128]{2,1,0:T(8,128)(2,1)S(1)}, u32[]{:S(2)}, u32[]{:S(2)}) collective-permute-start(bf16[2,32,128]{2,1,0:T(8,128)(2,1)S(1)} %iterate.1.refs_16_), channel_id=1, source_target_pairs={{0,7},{1,6},{2,5},{3,4},{4,3},{5,2},{6,1},{7,0},{8,15},{9,14},{10,... | collective-permute-start | bytes 49160 | tf_op jit(solution)/shard_map/ppermute | solution.py:254
  136.2 8.1 %collective-permute-start.33 = (bf16[2,32,128]{2,1,0:T(8,128)(2,1)S(1)}, bf16[2,32,128]{2,1,0:T(8,128)(2,1)S(1)}, u32[]{:S(2)}, u32[]{:S(2)}) collective-permute-start(bf16[2,32,128]{2,1,0:T(8,128)(2,1)S(1)} %iterate.1.refs_16_), channel_id=1, source_target_pairs={{0,6},{1,7},{2,4},{3,5},{4,2},{5,3},{6,0},{7,1},{8,14},{9,15},{10,... | collective-permute-start | bytes 49160 | tf_op jit(solution)/shard_map/ppermute | solution.py:254
  146.3 2.9 %collective-permute-start.31 = (bf16[2,32,128]{2,1,0:T(8,128)(2,1)S(1)}, bf16[2,32,128]{2,1,0:T(8,128)(2,1)S(1)}, u32[]{:S(2)}, u32[]{:S(2)}) collective-permute-start(bf16[2,32,128]{2,1,0:T(8,128)(2,1)S(1)} %iterate.1.refs_16_), channel_id=1, source_target_pairs={{0,4},{1,5},{2,6},{3,7},{4,0},{5,1},{6,2},{7,3},{8,12},{9,13},{10,... | collective-permute-start | bytes 49160 | tf_op jit(solution)/shard_map/ppermute | solution.py:254
  151.7 5.9 %collective-permute-start.29 = (bf16[2,32,128]{2,1,0:T(8,128)(2,1)S(1)}, bf16[2,32,128]{2,1,0:T(8,128)(2,1)S(1)}, u32[]{:S(2)}, u32[]{:S(2)}) collective-permute-start(bf16[2,32,128]{2,1,0:T(8,128)(2,1)S(1)} %iterate.1.refs_16_), channel_id=1, source_target_pairs={{0,2},{1,3},{2,0},{3,1},{4,6},{5,7},{6,4},{7,5},{8,10},{9,11},{10,... | collective-permute-start | bytes 49160 | tf_op jit(solution)/shard_map/ppermute | solution.py:254
  159.6 3.7 %collective-permute-done.28.refs_17_ = bf16[2,32,128]{2,1,0:T(8,128)(2,1)S(1)} collective-permute-done((bf16[2,32,128]{2,1,0:T(8,128)(2,1)S(1)}, bf16[2,32,128]{2,1,0:T(8,128)(2,1)S(1)}, u32[]{:S(2)}, u32[]{:S(2)}) %collective-permute-start.28) | collective-permute-done | bytes 16416 | tf_op jit(solution)/shard_map/ppermute | solution.py:254
  (61 shorter events, 46.7 us)
Async XLA Ops:
  5.7 16.5 %collective-permute-start.7 = (bf16[256,256]{1,0:T(8,128)(2,1)S(1)}, bf16[256,256]{1,0:T(8,128)(2,1)S(1)}, u32[]{:S(2)}, u32[]{:S(2)}) collective-permute-start(bf16[256,256]{1,0:T(8,128)(2,1)S(1)} %get-tuple-element.37), channel_id=1, source_target_pairs={{0,64},{64,0},{128,192},{192,128},{256,320},{320,256},{384,448},{4... | collective-permute-start | bytes 393224 | tf_op jit(solution)/shard_map/ppermute | solution.py:254
  7.7 19.5 %collective-permute-start.8 = (bf16[256,256]{1,0:T(8,128)(2,1)S(1)}, bf16[256,256]{1,0:T(8,128)(2,1)S(1)}, u32[]{:S(2)}, u32[]{:S(2)}) collective-permute-start(bf16[256,256]{1,0:T(8,128)(2,1)S(1)} %get-tuple-element.38), channel_id=1, source_target_pairs={{0,128},{64,192},{128,0},{192,64},{256,384},{320,448},{384,256},{4... | collective-permute-start | bytes 393224 | tf_op jit(solution)/shard_map/ppermute | solution.py:254
  11.2 18.0 %collective-permute-start.9 = (bf16[256,256]{1,0:T(8,128)(2,1)S(1)}, bf16[256,256]{1,0:T(8,128)(2,1)S(1)}, u32[]{:S(2)}, u32[]{:S(2)}) collective-permute-start(bf16[256,256]{1,0:T(8,128)(2,1)S(1)} %get-tuple-element.39), channel_id=1, source_target_pairs={{0,192},{64,128},{128,64},{192,0},{256,448},{320,384},{384,320},{4... | collective-permute-start | bytes 393224 | tf_op jit(solution)/shard_map/ppermute | solution.py:254
  13.3 18.0 %collective-permute-start.10 = (bf16[256,256]{1,0:T(8,128)(2,1)S(1)}, bf16[256,256]{1,0:T(8,128)(2,1)S(1)}, u32[]{:S(2)}, u32[]{:S(2)}) collective-permute-start(bf16[256,256]{1,0:T(8,128)(2,1)S(1)} %get-tuple-element.40), channel_id=1, source_target_pairs={{0,256},{64,320},{128,384},{192,448},{256,0},{320,64},{384,128},{4... | collective-permute-start | bytes 393224 | tf_op jit(solution)/shard_map/ppermute | solution.py:254
  18.5 15.2 %collective-permute-start.11 = (bf16[256,256]{1,0:T(8,128)(2,1)S(1)}, bf16[256,256]{1,0:T(8,128)(2,1)S(1)}, u32[]{:S(2)}, u32[]{:S(2)}) collective-permute-start(bf16[256,256]{1,0:T(8,128)(2,1)S(1)} %get-tuple-element.41), channel_id=1, source_target_pairs={{0,320},{64,256},{128,448},{192,384},{256,64},{320,0},{384,192},{4... | collective-permute-start | bytes 393224 | tf_op jit(solution)/shard_map/ppermute | solution.py:254
  22.3 14.5 %collective-permute-start.12 = (bf16[256,256]{1,0:T(8,128)(2,1)S(1)}, bf16[256,256]{1,0:T(8,128)(2,1)S(1)}, u32[]{:S(2)}, u32[]{:S(2)}) collective-permute-start(bf16[256,256]{1,0:T(8,128)(2,1)S(1)} %get-tuple-element.42), channel_id=1, source_target_pairs={{0,384},{64,448},{128,256},{192,320},{256,128},{320,192},{384,0},{... | collective-permute-start | bytes 393224 | tf_op jit(solution)/shard_map/ppermute | solution.py:254
  27.1 14.5 %collective-permute-start.13 = (bf16[256,256]{1,0:T(8,128)(2,1)S(1)}, bf16[256,256]{1,0:T(8,128)(2,1)S(1)}, u32[]{:S(2)}, u32[]{:S(2)}) collective-permute-start(bf16[256,256]{1,0:T(8,128)(2,1)S(1)} %get-tuple-element.43), channel_id=1, source_target_pairs={{0,448},{64,384},{128,320},{192,256},{256,192},{320,128},{384,64},... | collective-permute-start | bytes 393224 | tf_op jit(solution)/shard_map/ppermute | solution.py:254
  29.2 14.9 %collective-permute-start = (bf16[256,256]{1,0:T(8,128)(2,1)S(1)}, bf16[256,256]{1,0:T(8,128)(2,1)S(1)}, u32[]{:S(2)}, u32[]{:S(2)}) collective-permute-start(bf16[256,256]{1,0:T(8,128)(2,1)S(1)} %get-tuple-element.29), channel_id=1, source_target_pairs={{0,64},{64,0},{128,192},{192,128},{256,320},{320,256},{384,448},{4... | collective-permute-start | bytes 393224 | tf_op jit(solution)/shard_map/ppermute | solution.py:254
  31.4 17.6 %collective-permute-start.1 = (bf16[256,256]{1,0:T(8,128)(2,1)S(1)}, bf16[256,256]{1,0:T(8,128)(2,1)S(1)}, u32[]{:S(2)}, u32[]{:S(2)}) collective-permute-start(bf16[256,256]{1,0:T(8,128)(2,1)S(1)} %get-tuple-element.30), channel_id=1, source_target_pairs={{0,128},{64,192},{128,0},{192,64},{256,384},{320,448},{384,256},{4... | collective-permute-start | bytes 393224 | tf_op jit(solution)/shard_map/ppermute | solution.py:254
  33.6 17.3 %collective-permute-start.2 = (bf16[256,256]{1,0:T(8,128)(2,1)S(1)}, bf16[256,256]{1,0:T(8,128)(2,1)S(1)}, u32[]{:S(2)}, u32[]{:S(2)}) collective-permute-start(bf16[256,256]{1,0:T(8,128)(2,1)S(1)} %get-tuple-element.31), channel_id=1, source_target_pairs={{0,192},{64,128},{128,64},{192,0},{256,448},{320,384},{384,320},{4... | collective-permute-start | bytes 393224 | tf_op jit(solution)/shard_map/ppermute | solution.py:254
  36.8 14.1 %collective-permute-start.3 = (bf16[256,256]{1,0:T(8,128)(2,1)S(1)}, bf16[256,256]{1,0:T(8,128)(2,1)S(1)}, u32[]{:S(2)}, u32[]{:S(2)}) collective-permute-start(bf16[256,256]{1,0:T(8,128)(2,1)S(1)} %get-tuple-element.32), channel_id=1, source_target_pairs={{0,256},{64,320},{128,384},{192,448},{256,0},{320,64},{384,128},{4... | collective-permute-start | bytes 393224 | tf_op jit(solution)/shard_map/ppermute | solution.py:254
  59.3 19.0 %collective-permute-start.14 = (bf16[2,32,128]{2,1,0:T(8,128)(2,1)S(1)}, bf16[2,32,128]{2,1,0:T(8,128)(2,1)S(1)}, u32[]{:S(2)}, u32[]{:S(2)}) collective-permute-start(bf16[2,32,128]{2,1,0:T(8,128)(2,1)S(1)} %get-tuple-element.45), channel_id=1, source_target_pairs={{0,1},{1,0},{2,3},{3,2},{4,5},{5,4},{6,7},{7,6},{8,9},{9,8},{10,11... | collective-permute-start | bytes 49160 | tf_op jit(solution)/shard_map/ppermute | solution.py:254
  64.4 15.8 %collective-permute-start.15 = (bf16[2,32,128]{2,1,0:T(8,128)(2,1)S(1)}, bf16[2,32,128]{2,1,0:T(8,128)(2,1)S(1)}, u32[]{:S(2)}, u32[]{:S(2)}) collective-permute-start(bf16[2,32,128]{2,1,0:T(8,128)(2,1)S(1)} %get-tuple-element.46), channel_id=1, source_target_pairs={{0,2},{1,3},{2,0},{3,1},{4,6},{5,7},{6,4},{7,5},{8,10},{9,11},{10,... | collective-permute-start | bytes 49160 | tf_op jit(solution)/shard_map/ppermute | solution.py:254
  66.4 16.9 %collective-permute-start.16 = (bf16[2,32,128]{2,1,0:T(8,128)(2,1)S(1)}, bf16[2,32,128]{2,1,0:T(8,128)(2,1)S(1)}, u32[]{:S(2)}, u32[]{:S(2)}) collective-permute-start(bf16[2,32,128]{2,1,0:T(8,128)(2,1)S(1)} %get-tuple-element.47), channel_id=1, source_target_pairs={{0,3},{1,2},{2,1},{3,0},{4,7},{5,6},{6,5},{7,4},{8,11},{9,10},{10,... | collective-permute-start | bytes 49160 | tf_op jit(solution)/shard_map/ppermute | solution.py:254
  69.7 13.5 %collective-permute-start.17 = (bf16[2,32,128]{2,1,0:T(8,128)(2,1)S(1)}, bf16[2,32,128]{2,1,0:T(8,128)(2,1)S(1)}, u32[]{:S(2)}, u32[]{:S(2)}) collective-permute-start(bf16[2,32,128]{2,1,0:T(8,128)(2,1)S(1)} %get-tuple-element.48), channel_id=1, source_target_pairs={{0,4},{1,5},{2,6},{3,7},{4,0},{5,1},{6,2},{7,3},{8,12},{9,13},{10,... | collective-permute-start | bytes 49160 | tf_op jit(solution)/shard_map/ppermute | solution.py:254
  86.8 34.5 %collective-permute-start.27 = (bf16[2,32,128]{2,1,0:T(8,128)(2,1)S(1)}, bf16[2,32,128]{2,1,0:T(8,128)(2,1)S(1)}, u32[]{:S(2)}, u32[]{:S(2)}) collective-permute-start(bf16[2,32,128]{2,1,0:T(8,128)(2,1)S(1)} %total.1.refs_0_), channel_id=1, source_target_pairs={{0,56},{8,48},{16,40},{24,32},{32,24},{40,16},{48,8},{56,0},{1,57}... | collective-permute-start | bytes 49160 | tf_op jit(solution)/shard_map/ppermute | solution.py:254
  97.5 25.7 %collective-permute-start.26 = (bf16[2,32,128]{2,1,0:T(8,128)(2,1)S(1)}, bf16[2,32,128]{2,1,0:T(8,128)(2,1)S(1)}, u32[]{:S(2)}, u32[]{:S(2)}) collective-permute-start(bf16[2,32,128]{2,1,0:T(8,128)(2,1)S(1)} %total.1.refs_0_), channel_id=1, source_target_pairs={{0,48},{8,56},{16,32},{24,40},{32,16},{40,24},{48,0},{56,8},{1,49}... | collective-permute-start | bytes 49160 | tf_op jit(solution)/shard_map/ppermute | solution.py:254
  100.4 28.6 %collective-permute-start.25 = (bf16[2,32,128]{2,1,0:T(8,128)(2,1)S(1)}, bf16[2,32,128]{2,1,0:T(8,128)(2,1)S(1)}, u32[]{:S(2)}, u32[]{:S(2)}) collective-permute-start(bf16[2,32,128]{2,1,0:T(8,128)(2,1)S(1)} %total.1.refs_0_), channel_id=1, source_target_pairs={{0,40},{8,32},{16,56},{24,48},{32,8},{40,0},{48,24},{56,16},{1,41}... | collective-permute-start | bytes 49160 | tf_op jit(solution)/shard_map/ppermute | solution.py:254
  109.4 19.6 %collective-permute-start.24 = (bf16[2,32,128]{2,1,0:T(8,128)(2,1)S(1)}, bf16[2,32,128]{2,1,0:T(8,128)(2,1)S(1)}, u32[]{:S(2)}, u32[]{:S(2)}) collective-permute-start(bf16[2,32,128]{2,1,0:T(8,128)(2,1)S(1)} %total.1.refs_0_), channel_id=1, source_target_pairs={{0,32},{8,40},{16,48},{24,56},{32,0},{40,8},{48,16},{56,24},{1,33}... | collective-permute-start | bytes 49160 | tf_op jit(solution)/shard_map/ppermute | solution.py:254
  115.0 14.1 %collective-permute-start.23 = (bf16[2,32,128]{2,1,0:T(8,128)(2,1)S(1)}, bf16[2,32,128]{2,1,0:T(8,128)(2,1)S(1)}, u32[]{:S(2)}, u32[]{:S(2)}) collective-permute-start(bf16[2,32,128]{2,1,0:T(8,128)(2,1)S(1)} %total.1.refs_0_), channel_id=1, source_target_pairs={{0,24},{8,16},{16,8},{24,0},{32,56},{40,48},{48,40},{56,32},{1,25}... | collective-permute-start | bytes 49160 | tf_op jit(solution)/shard_map/ppermute | solution.py:254
  133.3 18.3 %collective-permute-start.34 = (bf16[2,32,128]{2,1,0:T(8,128)(2,1)S(1)}, bf16[2,32,128]{2,1,0:T(8,128)(2,1)S(1)}, u32[]{:S(2)}, u32[]{:S(2)}) collective-permute-start(bf16[2,32,128]{2,1,0:T(8,128)(2,1)S(1)} %iterate.1.refs_16_), channel_id=1, source_target_pairs={{0,7},{1,6},{2,5},{3,4},{4,3},{5,2},{6,1},{7,0},{8,15},{9,14},{10,... | collective-permute-start | bytes 49160 | tf_op jit(solution)/shard_map/ppermute | solution.py:254
  136.2 21.4 %collective-permute-start.33 = (bf16[2,32,128]{2,1,0:T(8,128)(2,1)S(1)}, bf16[2,32,128]{2,1,0:T(8,128)(2,1)S(1)}, u32[]{:S(2)}, u32[]{:S(2)}) collective-permute-start(bf16[2,32,128]{2,1,0:T(8,128)(2,1)S(1)} %iterate.1.refs_16_), channel_id=1, source_target_pairs={{0,6},{1,7},{2,4},{3,5},{4,2},{5,3},{6,0},{7,1},{8,14},{9,15},{10,... | collective-permute-start | bytes 49160 | tf_op jit(solution)/shard_map/ppermute | solution.py:254
  144.4 15.2 %collective-permute-start.32 = (bf16[2,32,128]{2,1,0:T(8,128)(2,1)S(1)}, bf16[2,32,128]{2,1,0:T(8,128)(2,1)S(1)}, u32[]{:S(2)}, u32[]{:S(2)}) collective-permute-start(bf16[2,32,128]{2,1,0:T(8,128)(2,1)S(1)} %iterate.1.refs_16_), channel_id=1, source_target_pairs={{0,5},{1,4},{2,7},{3,6},{4,1},{5,0},{6,3},{7,2},{8,13},{9,12},{10,... | collective-permute-start | bytes 49160 | tf_op jit(solution)/shard_map/ppermute | solution.py:254
  146.3 13.3 %collective-permute-start.31 = (bf16[2,32,128]{2,1,0:T(8,128)(2,1)S(1)}, bf16[2,32,128]{2,1,0:T(8,128)(2,1)S(1)}, u32[]{:S(2)}, u32[]{:S(2)}) collective-permute-start(bf16[2,32,128]{2,1,0:T(8,128)(2,1)S(1)} %iterate.1.refs_16_), channel_id=1, source_target_pairs={{0,4},{1,5},{2,6},{3,7},{4,0},{5,1},{6,2},{7,3},{8,12},{9,13},{10,... | collective-permute-start | bytes 49160 | tf_op jit(solution)/shard_map/ppermute | solution.py:254
  (15 other events, 308.8 us)

commit v6 on v4

--- a/solution.py
+++ b/solution.py
@@ -1,9 +1,8 @@
 import functools
+import math
 
 import jax
 import jax.numpy as jnp
-import ml_dtypes
-import numpy as np
 from jax import lax
 from jax.experimental import pallas as pl
 from jax.experimental.pallas import tpu as pltpu
@@ -17,16 +16,24 @@
 VMEM_LIMIT = 48 * 1024 * 1024
 
 
-def make_table(freqs, steps):
-    times = np.arange(steps)
-    phase = (np.arange(freqs)[:, None] * times[None, :]) % steps
-    angle = 2.0 * np.pi * phase / steps
-    window = np.sqrt(8.0 / (3.0 * steps)) * 0.5 * (1.0 - np.cos(2.0 * np.pi * times / steps))
-    table = np.stack([np.cos(angle) * window, np.sin(angle) * window], 1)
-    table = table.reshape(2 * freqs, steps).astype(np.float32)
-    high = table.astype(ml_dtypes.bfloat16)
-    low = (table - high.astype(np.float32)).astype(ml_dtypes.bfloat16)
-    return np.concatenate([high, low], 0)
+def sine(x):
+    square = x * x
+    total = jnp.full_like(x, 1.0 / math.factorial(13))
+    for n in (11, 9, 7, 5, 3, 1):
+        total = total * square + (1.0 if n % 4 == 1 else -1.0) / math.factorial(n)
+    return total * x
+
+
+def make_table(rows, steps):
+    row = lax.broadcasted_iota(jnp.int32, (rows, steps), 0)
+    time = lax.broadcasted_iota(jnp.int32, (rows, steps), 1)
+    phase = (row >> 1) * time - (row & 1) * (steps // 4)
+    phase = ((phase + steps // 2) & (steps - 1)) - steps // 2
+    half = sine(phase.astype(F32) * (math.pi / steps))
+    time = lax.broadcasted_iota(jnp.int32, (8, steps), 1)
+    window = sine((time - steps // 2).astype(F32) * (math.pi / steps))
+    window = math.sqrt(8.0 / (3.0 * steps)) * (1.0 - window * window)
+    return (1.0 - 2.0 * half * half) * window[:1]
 
 
 def split(x):
@@ -38,43 +45,43 @@
     return lax.dot_general(a, b, dims, preferred_element_type=F32, precision=precision)
 
 
-def dft_kernel(table_ref, x_ref, out_ref, spectra_ref):
-    blocks = x_ref.shape[0]
-    rows = table_ref.shape[0] // 2
-    table = table_ref[...]
-    high = table[:rows]
+def dft_kernel(x_ref, out_ref, table_ref, acc_ref):
+    blocks, steps = x_ref.shape[:2]
+    rows = table_ref.shape[0]
+
+    @pl.when(pl.program_id(0) == 0)
+    def _():
+        high, low = split(make_table(rows, steps))
+        table_ref[:, :steps] = high
+        table_ref[:, steps : 2 * steps] = low
+        table_ref[:, 2 * steps :] = high
+
     for b in range(blocks):
         xh, xl = split(x_ref[b])
-        both = mm(table, xh)
-        spectra_ref[b] = (both[:rows] + (both[rows:] + mm(high, xl))).astype(BF16)
-    size = 256
-    per = size // blocks
-    to = lax.broadcasted_iota(jnp.int32, (size, size), 0)
-    at = lax.broadcasted_iota(jnp.int32, (size, size), 1)
-    order = jnp.where((at % per) * blocks + at // per == to, 1.0, 0.0).astype(BF16)
-    for g in range(rows // per):
-        group = spectra_ref[:, g * per : (g + 1) * per].reshape(size, -1)
-        out_ref[g * size : (g + 1) * size] = mm(order, group).astype(BF16)
+        acc = mm(table_ref[...], jnp.concatenate([xh, xh, xl], 0))
+        for col in range(0, acc.shape[1], 128):
+            acc_ref[col // 128, pl.ds(b, rows, stride=blocks), :] = acc[:, col : col + 128]
+    for col in range(0, out_ref.shape[1], 128):
+        out_ref[:, col : col + 128] = acc_ref[col // 128].astype(BF16)
 
 
 def dft(snapshots, freqs):
     blocks, steps, pts = snapshots.shape
-    table = make_table(freqs, steps)
     wide = 256
     rows = 2 * freqs
     return pl.pallas_call(
         dft_kernel,
         grid=(pts // wide,),
-        in_specs=[
-            pl.BlockSpec((2 * rows, steps), lambda i: (0, 0)),
-            pl.BlockSpec((blocks, steps, wide), lambda i: (0, 0, i)),
-        ],
+        in_specs=[pl.BlockSpec((blocks, steps, wide), lambda i: (0, 0, i))],
         out_specs=pl.BlockSpec((rows * blocks, wide), lambda i: (0, i)),
         out_shape=jax.ShapeDtypeStruct((rows * blocks, pts), BF16),
-        scratch_shapes=[pltpu.VMEM((blocks, rows, wide), BF16)],
+        scratch_shapes=[
+            pltpu.VMEM((rows, 3 * steps), BF16),
+            pltpu.VMEM((wide // 128, rows * blocks, 128), F32),
+        ],
         compiler_params=pltpu.CompilerParams(vmem_limit_bytes=VMEM_LIMIT),
         name="dft",
-    )(jnp.asarray(table), snapshots)
+    )(snapshots)
 
 
 def exchange(x, sign_first):
@@ -130,20 +137,23 @@
         out_ref[i] = total
 
 
-def factor_out(image):
-    cross = mm(image, image, NT, lax.Precision.HIGHEST)
-    columns = [jnp.broadcast_to(cross[:, k : k + 1], image.shape) for k in range(KM)]
-    row = lax.broadcasted_iota(jnp.int32, image.shape, 0)
-    pivots = columns[KM - 1]
+def factor_out(images):
+    images = list(images)
+    every = range(len(images))
+    cross = [mm(x, x, NT, lax.Precision.HIGHEST) for x in images]
+    columns = [[jnp.broadcast_to(c[:, k : k + 1], (KM, 128)) for k in range(KM)] for c in cross]
+    row = lax.broadcasted_iota(jnp.int32, (KM, 128), 0)
+    pivots = [columns[f][KM - 1] for f in every]
     for k in range(KM):
-        pivot = columns[k][k : k + 1]
-        pivots = jnp.where(row == k, pivot, pivots)
-        if k < KM - 1:
-            factor = jnp.where(row > k, columns[k] * (1.0 / pivot), 0.0)
-            for j in range(k + 1, KM):
-                columns[j] = columns[j] - factor * columns[j][k : k + 1]
-            image = image - factor * image[k : k + 1]
-    return image * lax.rsqrt(pivots)
+        for f in every:
+            pivot = columns[f][k][k : k + 1]
+            pivots[f] = jnp.where(row == k, pivot, pivots[f])
+            if k < KM - 1:
+                factor = jnp.where(row > k, columns[f][k] * (1.0 / pivot), 0.0)
+                for j in range(k + 1, KM):
+                    columns[f][j] = columns[f][j] - factor * columns[f][j][k : k + 1]
+                images[f] = images[f] - factor * images[f][k : k + 1]
+    return [x * lax.rsqrt(p) for x, p in zip(images, pivots)]
 
 
 def unpacked(s):
@@ -161,39 +171,36 @@
     return jnp.stack([top.reshape(tall), bottom.reshape(tall)], 1).reshape(2 * rows, 128), top
 
 
-def iterate(s):
-    embedded, top = unpacked(s)
-    eh, el = split(embedded)
-    e = jnp.concatenate([eh, el], 1)
-
-    def times_e(basis):
-        high, low = split(basis)
-        r = mm(jnp.concatenate([high, low], 0), e)
-        return r[:KM, :128], r[KM:, :128] + r[:KM, 128:]
-
-    image = sum(times_e(top[:KM]))
-    basis = factor_out(image)
-    basis = factor_out(sum(times_e(sum(times_e(basis)))))
-    high, low = split(basis)
-    r = mm(jnp.concatenate([high, low], 0), e)
-    e_coef = r[:KM, :128] + r[:KM, 128:]
-    e_basis = e_coef + r[KM:, :128]
-    energy = jnp.sum(high.astype(F32) * e_coef, 1, keepdims=True)
-    quotient = jnp.sum(basis * e_basis, 1, keepdims=True)
-    lane = lax.broadcasted_iota(jnp.int32, (KM, 128), 1)
-    rest = jnp.where(lane < 3, lax.rsqrt(jnp.maximum(energy, 0.0) + 1e-06), quotient)
-    first = rest.astype(BF16).astype(F32)
-    second = (rest - first).astype(BF16).astype(F32)
-    third = rest - first - second
-    step = jnp.where(lane < 3, lane, lane - 3)
-    words = jnp.where(step == 0, first, jnp.where(step == 1, second, third))
-    return jnp.concatenate([high, jnp.where(lane < 6, words, 0.0).astype(BF16)], 0)
-
-
 def iterate_kernel(x_ref, out_ref):
     total = jnp.sum(x_ref[...].astype(F32), 0)
-    for f in range(x_ref.shape[1]):
-        result = iterate(total[f])
+    every = range(total.shape[0])
+    e, starts = [], []
+    for f in every:
+        embedded, top = unpacked(total[f])
+        e.append(jnp.concatenate(split(embedded), 1))
+        starts.append(top[:KM])
+
+    def products(basis):
+        r = [mm(jnp.concatenate(split(x), 0), e[f]) for f, x in enumerate(basis)]
+        return [(x[:KM, :128], x[KM:, :128], x[:KM, 128:]) for x in r]
+
+    def times_e(basis):
+        return [a + (b + c) for a, b, c in products(basis)]
+
+    basis = factor_out(times_e(starts))
+    basis = factor_out(times_e(times_e(basis)))
+    lane = lax.broadcasted_iota(jnp.int32, (KM, 128), 1)
+    for f, (a, b, c) in enumerate(products(basis)):
+        high = basis[f].astype(BF16)
+        energy = jnp.sum(high.astype(F32) * (a + c), 1, keepdims=True)
+        quotient = jnp.sum(basis[f] * (a + (b + c)), 1, keepdims=True)
+        rest = jnp.where(lane < 3, lax.rsqrt(jnp.maximum(energy, 0.0) + 1e-06), quotient)
+        first = rest.astype(BF16).astype(F32)
+        second = (rest - first).astype(BF16).astype(F32)
+        third = rest - first - second
+        step = jnp.where(lane < 3, lane, lane - 3)
+        words = jnp.where(step == 0, first, jnp.where(step == 1, second, third))
+        result = jnp.concatenate([high, jnp.where(lane < 6, words, 0.0).astype(BF16)], 0)
         for i in range(out_ref.shape[0]):
             out_ref[i, f] = result
 

time: 92.6 us -> 90.6 us (0.978)
  Pallas kernels: 10.4 us -> 9.41 us
  local copies, waits for them, and re-layouts: 0.96 us -> 0.01 us
    pallas_call x4, Pallas kernels: 5.9 us -> 4.89 us  [call(): pl.pallas_call(kernel, in_specs=[smem if x.dtype == jnp.int32 else vmem f...]
    unnamed x6 -> x4, local copies, waits for them, and re-layouts: 0.96 us -> 0.01 us
where the time goes in v6:
time: 90.6 us; the launch traced here: 90.4 us
  blocking collectives  80.3 us (89%)
  Pallas kernels  9.41 us (10%)
    all_to_all x1, blocking collectives, local(): lax.all_to_all(spectra, 'blk', split_axis=0, concat_axis=0, tiled=True)  31.8 us
    all_to_all x1, blocking collectives, local(): lax.all_to_all(copies, far, split_axis=0, concat_axis=0, tiled=True)  27.7 us
    all_to_all x1, blocking collectives, local(): parts = lax.all_to_all(parts, near, split_axis=0, concat_axis=0, tiled=True)  11.5 us
    all_to_all x1, blocking collectives, local(): coefs = lax.all_to_all(mine, near, split_axis=0, concat_axis=0, tiled=True)  9.31 us
    pallas_call x4, Pallas kernels, call(): pl.pallas_call(kernel, in_specs=[smem if x.dtype == jnp.int32 else vmem f...  4.89 us
    pallas_call x1, Pallas kernels, dft(): pl.pallas_call(dft_kernel, grid=(pts // wide,), in_specs=[pl.BlockSpec((b...  4.52 us

profile of v6, /device:TPU:2, one launch (start us, length us, event | category | flops | bytes accessed | tf_op | source)
XLA Modules:
  0.0 90.4 jit_solution(2358878160446029000)
XLA Ops:
  0.6 4.5 %dft.1 = bf16[2048,512]{1,0:T(8,128)(2,1)S(1)} custom-call(f32[8,256,512]{2,1,0:T(8,128)} %x_ref.1), custom_call_target="tpu_custom_call" | custom-call | tf_op jit(solution)/shard_map/dft/pallas_call | solution.py:72
  5.2 0.0 copy-start
  5.2 31.8 %all_to_all.20.z_ref = bf16[8,16,16,512]{3,2,1,0:T(8,128)(2,1)S(1)} all-to-all(bf16[8,16,16,512]{3,2,1,0:T(8,128)(2,1)S(1)} %bitcast.5), channel_id=1, replica_groups=mesh['blk'=8,'far'=8,'near'=2,'x'=4] {'blk'}, dimensions={0} | all-to-all | bytes 4194304 | tf_op jit(solution)/shard_map/all_to_all | solution.py:236
  37.0 0.0 copy-start.1
  37.0 0.0 copy-done
  37.0 1.1 %gram.1 = bf16[16,32,128]{2,1,0:T(8,128)(2,1)S(1)} custom-call(bf16[8,16,16,512]{3,2,1,0:T(8,128)(2,1)S(1)} %all_to_all.20.z_ref, f32[1,512]{1,0:T(1,128)S(1)} %bitcast.8), custom_call_target="tpu_custom_call" | custom-call | tf_op jit(solution)/shard_map/gram/pallas_call | solution.py:123
  38.0 11.5 %all_to_all.21.x_ref = bf16[8,2,32,128]{3,2,1,0:T(8,128)(2,1)S(1)} all-to-all(bf16[8,2,32,128]{3,2,1,0:T(8,128)(2,1)S(1)} %bitcast.7), channel_id=1, replica_groups=mesh['blk'=8,'far'=8,'near'=2,'x'=4] {'near','x'}, dimensions={0} | all-to-all | bytes 262144 | tf_op jit(solution)/shard_map/all_to_all | solution.py:247
  49.6 27.7 %all_to_all.22.x_ref = bf16[8,2,32,128]{3,2,1,0:T(8,128)(2,1)S(1)} all-to-all(bf16[8,2,32,128]{3,2,1,0:T(8,128)(2,1)S(1)} %total.1), channel_id=1, replica_groups=mesh['blk'=8,'far'=8,'near'=2,'x'=4] {'far'}, dimensions={0} | all-to-all | bytes 262144 | tf_op jit(solution)/shard_map/all_to_all | solution.py:249
  77.2 1.9 %iterate.1 = bf16[8,2,32,128]{3,2,1,0:T(8,128)(2,1)S(1)} custom-call(bf16[8,2,32,128]{3,2,1,0:T(8,128)(2,1)S(1)} %all_to_all.22.x_ref), custom_call_target="tpu_custom_call" | custom-call | tf_op jit(solution)/shard_map/iterate/pallas_call | solution.py:123
  79.1 9.3 %all_to_all.23 = bf16[8,2,32,128]{3,2,1,0:T(8,128)(2,1)S(1)} all-to-all(bf16[8,2,32,128]{3,2,1,0:T(8,128)(2,1)S(1)} %iterate.1), channel_id=1, replica_groups=mesh['blk'=8,'far'=8,'near'=2,'x'=4] {'near','x'}, dimensions={0} | all-to-all | bytes 262144 | tf_op jit(solution)/shard_map/all_to_all | solution.py:251
  88.4 0.0 copy-done.1
  88.4 1.9 %modes.1 = (bf16[16,32,512]{2,1,0:T(8,128)(2,1)}, f32[16,16]{1,0:T(8,128)}) custom-call(s32[16]{0:T(128)S(1)} %copy-done.1, bf16[16,32,128]{2,1,0:T(8,128)(2,1)S(1)} %bitcast.6, bf16[8,16,16,512]{3,2,1,0:T(8,128)(2,1)S(1)} %all_to_all.20.z_ref), custom_call_target="tpu_custom_call" | custom-call | tf_op jit(solution)/shard_map/modes/pallas_call | solution.py:123
  (1 shorter events, 0.0 us)
Async XLA Ops:
  5.2 31.8 %copy-start = (f32[512]{0:T(512)S(1)}, f32[512]{0:T(512)}, u32[]{:S(2)}) copy-start(f32[512]{0:T(512)} %param.4) | copy-start | bytes 6148
  37.0 51.5 %copy-start.1 = (s32[16]{0:T(128)S(1)}, s32[16]{0:T(128)}, u32[]{:S(2)}) copy-start(s32[16]{0:T(128)} %counts_ref.1) | copy-start | bytes 196

commit v7 on v6

--- a/solution.py
+++ b/solution.py
@@ -45,24 +45,30 @@
     return lax.dot_general(a, b, dims, preferred_element_type=F32, precision=precision)
 
 
-def dft_kernel(x_ref, out_ref, table_ref, acc_ref):
-    blocks, steps = x_ref.shape[:2]
+def dft_kernel(x_hbm, out_ref, table_ref, acc_ref, x_ref, sems):
+    blocks, steps, pts = x_hbm.shape
     rows = table_ref.shape[0]
-
-    @pl.when(pl.program_id(0) == 0)
-    def _():
-        high, low = split(make_table(rows, steps))
-        table_ref[:, :steps] = high
-        table_ref[:, steps : 2 * steps] = low
-        table_ref[:, 2 * steps :] = high
-
-    for b in range(blocks):
-        xh, xl = split(x_ref[b])
-        acc = mm(table_ref[...], jnp.concatenate([xh, xh, xl], 0))
-        for col in range(0, acc.shape[1], 128):
-            acc_ref[col // 128, pl.ds(b, rows, stride=blocks), :] = acc[:, col : col + 128]
-    for col in range(0, out_ref.shape[1], 128):
-        out_ref[:, col : col + 128] = acc_ref[col // 128].astype(BF16)
+    parts, wide = x_ref.shape[0], x_ref.shape[3]
+    fetches = [
+        pltpu.make_async_copy(x_hbm.at[:, :, pl.ds(i * wide, wide)], x_ref.at[i], sems.at[i])
+        for i in range(parts)
+    ]
+    for fetch in fetches:
+        fetch.start()
+    high, low = split(make_table(rows, steps))
+    table_ref[:, :steps] = high
+    table_ref[:, steps : 2 * steps] = low
+    table_ref[:, 2 * steps :] = high
+    for i in range(parts):
+        fetches[i].wait()
+        for b in range(blocks):
+            xh, xl = split(x_ref[i, b])
+            acc = mm(table_ref[...], jnp.concatenate([xh, xh, xl], 0))
+            for col in range(0, wide, 128):
+                acc_ref[col // 128, pl.ds(b, rows, stride=blocks), :] = acc[:, col : col + 128]
+        for col in range(0, wide, 128):
+            at = i * wide + col
+            out_ref[:, at : at + 128] = acc_ref[col // 128].astype(BF16)
 
 
 def dft(snapshots, freqs):
@@ -71,13 +77,14 @@
     rows = 2 * freqs
     return pl.pallas_call(
         dft_kernel,
-        grid=(pts // wide,),
-        in_specs=[pl.BlockSpec((blocks, steps, wide), lambda i: (0, 0, i))],
-        out_specs=pl.BlockSpec((rows * blocks, wide), lambda i: (0, i)),
+        in_specs=[pl.BlockSpec(memory_space=pl.ANY)],
+        out_specs=pl.BlockSpec(memory_space=pltpu.VMEM),
         out_shape=jax.ShapeDtypeStruct((rows * blocks, pts), BF16),
         scratch_shapes=[
             pltpu.VMEM((rows, 3 * steps), BF16),
             pltpu.VMEM((wide // 128, rows * blocks, 128), F32),
+            pltpu.VMEM((pts // wide, blocks, steps, wide), F32),
+            pltpu.SemaphoreType.DMA((pts // wide,)),
         ],
         compiler_params=pltpu.CompilerParams(vmem_limit_bytes=VMEM_LIMIT),
         name="dft",

time: 90.6 us -> 90.2 us (level)
  no operation moved by 1% of the time
where the time goes in v7:
time: 90.2 us; the launch traced here: 90 us
  blocking collectives  80.3 us (89%)
  Pallas kernels  9.03 us (10%)
    all_to_all x1, blocking collectives, local(): lax.all_to_all(spectra, 'blk', split_axis=0, concat_axis=0, tiled=True)  31.8 us
    all_to_all x1, blocking collectives, local(): lax.all_to_all(copies, far, split_axis=0, concat_axis=0, tiled=True)  27.7 us
    all_to_all x1, blocking collectives, local(): parts = lax.all_to_all(parts, near, split_axis=0, concat_axis=0, tiled=True)  11.5 us
    all_to_all x1, blocking collectives, local(): coefs = lax.all_to_all(mine, near, split_axis=0, concat_axis=0, tiled=True)  9.31 us
    pallas_call x4, Pallas kernels, call(): pl.pallas_call(kernel, in_specs=[smem if x.dtype == jnp.int32 else vmem f...  4.89 us
    pallas_call x1, Pallas kernels, dft(): pl.pallas_call(dft_kernel, in_specs=[pl.BlockSpec(memory_space=pl.ANY)],...  4.14 us

profile of v7, /device:TPU:2, one launch (start us, length us, event | category | flops | bytes accessed | tf_op | source)
XLA Modules:
  0.0 90.0 jit_solution(18222757237639531974)
XLA Ops:
  0.6 4.1 %dft.1 = bf16[2048,512]{1,0:T(8,128)(2,1)S(1)} custom-call(f32[8,256,512]{2,1,0:T(8,128)} %x_hbm.1), custom_call_target="tpu_custom_call" | custom-call | tf_op jit(solution)/shard_map/dft/pallas_call | solution.py:78
  4.8 0.0 copy-start
  4.8 31.8 %all_to_all.20.z_ref = bf16[8,16,16,512]{3,2,1,0:T(8,128)(2,1)S(1)} all-to-all(bf16[8,16,16,512]{3,2,1,0:T(8,128)(2,1)S(1)} %bitcast.5), channel_id=1, replica_groups=mesh['blk'=8,'far'=8,'near'=2,'x'=4] {'blk'}, dimensions={0} | all-to-all | bytes 4194304 | tf_op jit(solution)/shard_map/all_to_all | solution.py:243
  36.6 0.0 copy-start.1
  36.6 0.0 copy-done
  36.6 1.1 %gram.1 = bf16[16,32,128]{2,1,0:T(8,128)(2,1)S(1)} custom-call(bf16[8,16,16,512]{3,2,1,0:T(8,128)(2,1)S(1)} %all_to_all.20.z_ref, f32[1,512]{1,0:T(1,128)S(1)} %bitcast.8), custom_call_target="tpu_custom_call" | custom-call | tf_op jit(solution)/shard_map/gram/pallas_call | solution.py:130
  37.6 11.5 %all_to_all.21.x_ref = bf16[8,2,32,128]{3,2,1,0:T(8,128)(2,1)S(1)} all-to-all(bf16[8,2,32,128]{3,2,1,0:T(8,128)(2,1)S(1)} %bitcast.7), channel_id=1, replica_groups=mesh['blk'=8,'far'=8,'near'=2,'x'=4] {'near','x'}, dimensions={0} | all-to-all | bytes 262144 | tf_op jit(solution)/shard_map/all_to_all | solution.py:254
  49.2 27.7 %all_to_all.22.x_ref = bf16[8,2,32,128]{3,2,1,0:T(8,128)(2,1)S(1)} all-to-all(bf16[8,2,32,128]{3,2,1,0:T(8,128)(2,1)S(1)} %total.1), channel_id=1, replica_groups=mesh['blk'=8,'far'=8,'near'=2,'x'=4] {'far'}, dimensions={0} | all-to-all | bytes 262144 | tf_op jit(solution)/shard_map/all_to_all | solution.py:256
  76.8 1.9 %iterate.1 = bf16[8,2,32,128]{3,2,1,0:T(8,128)(2,1)S(1)} custom-call(bf16[8,2,32,128]{3,2,1,0:T(8,128)(2,1)S(1)} %all_to_all.22.x_ref), custom_call_target="tpu_custom_call" | custom-call | tf_op jit(solution)/shard_map/iterate/pallas_call | solution.py:130
  78.7 9.3 %all_to_all.23 = bf16[8,2,32,128]{3,2,1,0:T(8,128)(2,1)S(1)} all-to-all(bf16[8,2,32,128]{3,2,1,0:T(8,128)(2,1)S(1)} %iterate.1), channel_id=1, replica_groups=mesh['blk'=8,'far'=8,'near'=2,'x'=4] {'near','x'}, dimensions={0} | all-to-all | bytes 262144 | tf_op jit(solution)/shard_map/all_to_all | solution.py:258
  88.0 0.0 copy-done.1
  88.0 1.9 %modes.1 = (bf16[16,32,512]{2,1,0:T(8,128)(2,1)}, f32[16,16]{1,0:T(8,128)}) custom-call(s32[16]{0:T(128)S(1)} %copy-done.1, bf16[16,32,128]{2,1,0:T(8,128)(2,1)S(1)} %bitcast.6, bf16[8,16,16,512]{3,2,1,0:T(8,128)(2,1)S(1)} %all_to_all.20.z_ref), custom_call_target="tpu_custom_call" | custom-call | tf_op jit(solution)/shard_map/modes/pallas_call | solution.py:130
  (1 shorter events, 0.0 us)
Async XLA Ops:
  4.8 31.8 %copy-start = (f32[512]{0:T(512)S(1)}, f32[512]{0:T(512)}, u32[]{:S(2)}) copy-start(f32[512]{0:T(512)} %param.4) | copy-start | bytes 6148
  36.6 51.5 %copy-start.1 = (s32[16]{0:T(128)S(1)}, s32[16]{0:T(128)}, u32[]{:S(2)}) copy-start(s32[16]{0:T(128)} %counts_ref.1) | copy-start | bytes 196
